TPU v7x, 32 devices: a whole 2x2x4 slice. The times are simulated.
32 devices in a mesh: section: 2 (over x), fsdp: 16 (over z, y, core).
Axes of the slice: x: 2, y: 2, z: 4, core: 2. Of those that a mesh axis runs over, the one named last changes fastest.
Arguments:
- inputs: bfloat16 [2, 4096, 8192], P('section', 'fsdp'), may hold values from -6 to 6
- out_grad: bfloat16 [2, 4096, 512], P('section', 'fsdp'), may hold values from -6 to 6
- gain: float32 [2, 8192], P('section'), may hold values from 0.1 to 1.9
- tiles: bfloat16 [2, 192, 128, 128], P('section', 'fsdp'), may hold values from -1 to 1
- tile_rows: int32 [2, 192], P('section', 'fsdp'), may hold values from -1 to 63, as said below
- tile_cols: int32 [2, 192], P('section', 'fsdp'), may hold values from -1 to 3, as said below
Outputs:
- weight_grad: float32 [2, 192, 128, 128], P('section', 'fsdp')
- gain_grad: float32 [2, 8192], P('section', 'fsdp')
- upstream_grad: bfloat16 [2, 4096, 8192], P('section', 'fsdp')
Inputs may be any that keep to these rules, and one draw needn't show every extreme that they name: `tile_rows`: in each section the lists name 128 distinct blocks, one per used slot; an unused slot holds -1 in both lists. The 12 slots of one fsdp index hold its blocks first; in every draw half of the fsdp indices hold 12 blocks and the others a third as many. `tile_cols`: column blocks of the slots named in tile_rows; -1 exactly where tile_rows is -1.
All inputs are finite; a program needn't handle non-finite values.
Results may differ from a plain program's by a relative error of at most 0.0029.
Values may be sent and summed in bfloat16 or wider, within the bound.
A program may use at most 192 MiB of HBM per device.

v0:
```python
import jax
import jax.numpy as jnp
from jax import lax
from jax.sharding import PartitionSpec as P

EPS = 1e-05


def from_behind(value, axis, steps):
    count = lax.axis_size(axis)
    pairs = [(source, (source + steps) % count) for source in range(count)]
    return lax.ppermute(value, axis, pairs)


def on_device(inputs, out_grad, gain, tiles, tile_rows, tile_cols):
    activations = inputs[0]
    key_grads = out_grad[0]
    gain_row = gain[0]
    own_tiles = tiles[0]
    tokens_here, width = activations.shape
    side = own_tiles.shape[-1]
    row_blocks = width // side
    col_blocks = key_grads.shape[1] // side
    all_rows, all_cols = (
        lax.all_gather(tile_rows[0], "fsdp", axis=0, tiled=True),
        lax.all_gather(tile_cols[0], "fsdp", axis=0, tiled=True),
    )
    wide = activations.astype(jnp.float32)
    rstd = lax.rsqrt(jnp.mean(wide * wide, axis=-1, keepdims=True) + EPS)
    normed = wide * rstd
    scaled = (normed * gain_row).astype(jnp.bfloat16)
    grad_blocks = key_grads.reshape(tokens_here, col_blocks, side)
    scaled_blocks = scaled.reshape(tokens_here, row_blocks, side)
    start_total = jnp.zeros((tokens_here, row_blocks, side), jnp.float32)
    row_part = all_rows
    col_part = all_cols
    valid = row_part >= 0
    chosen = jnp.take(grad_blocks, jnp.where(valid, col_part, 0), axis=1)
    product = jnp.einsum(
        "mkj,kij->mki",
        chosen,
        lax.all_gather(own_tiles, "fsdp", axis=0, tiled=True),
        preferred_element_type=jnp.float32,
    )
    product = product * valid[None, :, None].astype(jnp.float32)
    feature_grad = (
        start_total.at[:, jnp.where(valid, row_part, 0)].add(product).reshape(tokens_here, width)
    )
    gain_terms = jnp.sum(feature_grad * normed, axis=0)
    gained = feature_grad * gain_row
    input_grad = (
        rstd * (gained - normed * jnp.mean(gained * normed, axis=-1, keepdims=True))
    ).astype(jnp.bfloat16)
    row_part = all_rows
    col_part = all_cols
    valid = row_part >= 0
    left = jnp.take(scaled_blocks, jnp.where(valid, row_part, 0), axis=1)
    right = jnp.take(grad_blocks, jnp.where(valid, col_part, 0), axis=1)
    summed = jnp.einsum("mki,mkj->kij", left, right, preferred_element_type=jnp.float32)
    weight_grad = lax.psum_scatter(
        summed * valid[:, None, None].astype(jnp.float32), "fsdp", scatter_dimension=0, tiled=True
    )
    upstream_grad = from_behind(input_grad, "section", -1)
    share = width // lax.axis_size("fsdp")
    gain_whole = lax.psum(gain_terms, "fsdp")
    gain_share = lax.dynamic_slice_in_dim(gain_whole, lax.axis_index("fsdp") * share, share)
    return (weight_grad[None], gain_share[None], upstream_grad[None])


def solution(mesh):
    in_specs = (
        P("section", "fsdp", None),
        P("section", "fsdp", None),
        P("section", None),
        P("section", "fsdp", None, None),
        P("section", "fsdp"),
        P("section", "fsdp"),
    )
    out_specs = (P("section", "fsdp", None, None), P("section", "fsdp"), P("section", "fsdp", None))
    return jax.shard_map(
        on_device, mesh=mesh, in_specs=in_specs, out_specs=out_specs, check_vma=False
    )
```

profile of v0, /device:TPU:0, one launch (start us, length us, event | category | flops | bytes accessed | tf_op | source)
XLA Modules:
  0.0 329.8 jit_solution(579768822471313728)
XLA Ops:
  7.2 0.0 all-gather.5.cloned.1.call-start
  7.2 0.7 all-gather.5.cloned.1.call-update
  7.9 0.0 reduce-scatter.2.cloned.1.call-start
  8.0 1.1 copy.24
  9.0 0.2 copy.25
  9.2 6.4 %copy.22 = bf16[1,256,8192]{1,2,0:T(8,128)(2,1)} copy(bf16[1,256,8192]{2,1,0:T(8,128)(2,1)} %param.8) | data formatting | bytes 8388608 | tf_op args[0]
  15.6 0.0 copy-start.3
  15.6 0.0 copy-start.1
  15.6 0.0 copy-start.2
  15.6 7.1 %copy.23 = f32[256,64,128]{2,0,1:T(8,128)} copy(bf16[256,64,128]{0,2,1:T(8,128)(2,1)} %bitcast.49) | data formatting | bytes 12582912 | tf_op jit(solution)/shard_map/convert_element_type | solution.py:28
  22.7 0.0 copy-done.3
  22.7 0.6 dynamic-slice
  23.9 0.0 copy-done.1
  23.9 0.1 bitcast_dynamic-update-slice_fusion
  24.0 0.0 copy-done.2
  24.0 0.1 bitcast_dynamic-update-slice_fusion.1
  24.1 13.9 %all-reduce.2 = (s32[192]{0:T(256)S(1)}, s32[192]{0:T(256)S(1)}) all-reduce(s32[192]{0:T(256)S(1)} %bitcast_dynamic-update-slice_fusion.1, s32[192]{0:T(256)S(1)} %bitcast_dynamic-update-slice_fusion), channel_id=2, replica_groups=mesh['section'=2,'fsdp'=16] {'fsdp'}, use_global_device_ids=true, to_apply=%add | all-reduce | flops 384 | bytes 3072 | tf_op jit(solution)/shard_map/all_gather | solution.py:25
  38.1 8.1 %gather_fusion.1 = bf16[192,256,128]{2,1,0:T(8,128)(2,1)} fusion(bf16[256,4,128]{2,0,1:T(8,128)(2,1)S(1)} %copy.25, s32[1024]{0:T(1024)S(1)} %pad_clamp_fusion), kind=kCustom, calls=%fused_computation.clone | custom fusion | bytes 25166592 | tf_op jit(solution)/shard_map/jit(_take)/gather | solution.py:58
  46.2 3.3 %fusion.10 = f32[256]{0:T(256)S(1)} fusion(bf16[1,256,8192]{1,2,0:T(8,128)(2,1)} %copy.22), kind=kLoop, calls=%fused_computation.18 | loop fusion | flops 6291200 | bytes 4195328 | tf_op jit(solution)/shard_map/reduce_sum | solution.py:29
  49.5 25.3 %all-gather.5.cloned.1.call-done = bf16[1,192,128,128]{3,2,0,1:T(8,128)(2,1)} async-done(((bf16[1,12,128,128]{3,2,0,1:T(8,128)(2,1)}), bf16[1,192,128,128]{3,2,0,1:T(8,128)(2,1)}) %all-gather.5.cloned.1.call-update) | async-done | bytes 6291472 | tf_op jit(solution)/shard_map/all_gather | solution.py:42
  74.8 18.1 %broadcast_multiply_fusion = f32[192,256,128]{2,1,0:T(8,128)} fusion(f32[192]{0:T(256)S(1)} %get-tuple-element.22, bf16[1,192,128,128]{3,2,0,1:T(8,128)(2,1)} %all-gather.5.cloned.1.call-done, bf16[192,256,128]{2,1,0:T(8,128)(2,1)} %gather_fusion.1, pred[192]{0:T(512)(128)(4,1)S(1)} %get-tuple-element.23), kind=kOutput, calls=%fused_computation.9 | convolution fusion | flops 1623195648 | bytes 44041152 | tf_op jit(solution)/shard_map/mkj,kij->mki/dot_general | solution.py:39
  93.0 4.3 %broadcast_in_dim.47 = f32[256,64,128]{2,0,1:T(8,128)} broadcast(f32[]{:T(128)} %constant.16.clone.1), dimensions={} | broadcast | bytes 8388612 | tf_op jit(solution)/shard_map/broadcast_in_dim | solution.py:34
  97.3 0.0 copy-start
  97.3 56.4 %scatter_fusion = f32[256,64,128]{2,0,1:T(8,128)} fusion(f32[256,64,128]{2,0,1:T(8,128)} %broadcast_in_dim.47, s32[192]{0:T(256)S(1)} %get-tuple-element.18, f32[192,256,128]{2,1,0:T(8,128)} %broadcast_multiply_fusion), kind=kCustom, calls=%fused_computation.2 | custom fusion | flops 6291456 | bytes 75498240 | tf_op jit(solution)/shard_map/scatter-add | solution.py:47
  153.7 0.0 copy-done
  153.7 9.5 %multiply_reduce_fusion = (f32[256]{0:T(256)S(1)}, f32[64,128]{1,0:T(8,128)S(1)}, bf16[256,64,128]{2,0,1:T(8,128)(2,1)}) fusion(f32[256,64,128]{2,0,1:T(8,128)} %scatter_fusion, f32[256,64,128]{2,0,1:T(8,128)} %copy.23, f32[64,128]{1,0:T(8,128)S(1)} %bitcast.52, f32[256]{0:T(256)S(1)} %add_rsqrt_fusion), kind=kLoop, calls=%fused_computation.20 | loop fusion | flops 16768768 | bytes 21039104 | tf_op jit(solution)/shard_map/reduce_sum | solution.py:52
  163.2 10.3 %gather_fusion = bf16[192,256,128]{2,1,0:T(8,128)(2,1)} fusion(bf16[256,64,128]{2,0,1:T(8,128)(2,1)} %get-tuple-element.21, s32[1024]{0:T(1024)S(1)} %pad_clamp_fusion.1), kind=kCustom, calls=%fused_computation.1 | custom fusion | bytes 25166592 | tf_op jit(solution)/shard_map/jit(_take)/gather | solution.py:57
  173.5 13.9 %broadcast_multiply_fusion.1 = f32[192,128,128]{2,1,0:T(8,128)} fusion(f32[192]{0:T(256)S(1)} %get-tuple-element.22, bf16[192,256,128]{2,1,0:T(8,128)(2,1)} %gather_fusion.1, pred[192]{0:T(512)(128)(4,1)S(1)} %get-tuple-element.23, bf16[192,256,128]{2,1,0:T(8,128)(2,1)} %gather_fusion, pred[192]{0:T(512)(128)(4,1)S(1)} %get-tuple-element.17), kind=kOutput, calls=%fused_computation.25 | convolution fusion | flops 1626341376 | bytes 37749888 | tf_op jit(solution)/shard_map/mki,mkj->kij/dot_general | solution.py:59
  187.4 0.0 reduce-scatter.2.cloned.1.call-update
  187.4 9.2 %copy.28 = f32[256,64,128]{0,2,1:T(8,128)} copy(f32[256,64,128]{2,0,1:T(8,128)} %scatter_fusion) | data formatting | bytes 16777216 | tf_op jit(solution)/shard_map/scatter-add | solution.py:47
  196.6 9.3 %fusion.9 = bf16[256,8192]{0,1:T(8,128)(2,1)} fusion(f32[256,64,128]{0,2,1:T(8,128)} %copy.28, bf16[1,256,8192]{1,2,0:T(8,128)(2,1)} %copy.22, f32[256]{0:T(256)S(1)} %broadcast_multiply_fusion.2, f32[8192]{0:T(1024)S(1)} %bitcast.53, f32[256]{0:T(256)S(1)} %add_rsqrt_fusion), kind=kLoop, calls=%fused_computation.15 | loop fusion | flops 14680064 | bytes 16812032 | tf_op jit(solution)/shard_map/convert_element_type | solution.py:53
  205.9 1.4 collective-permute-start
  207.3 62.5 %psum.7 = f32[8192]{0:T(1024)S(1)} all-reduce(f32[8192]{0:T(1024)S(1)} %bitcast.54), channel_id=1, replica_groups=mesh['section'=2,'fsdp'=16] {'fsdp'}, use_global_device_ids=true, to_apply=%region_4.6 | all-reduce | flops 8192 | bytes 65536 | tf_op jit(solution)/shard_map/psum | solution.py:65
  269.9 0.7 dynamic_slice.3
  270.5 28.5 %collective-permute-done = bf16[256,8192]{0,1:T(8,128)(2,1)} collective-permute-done((bf16[256,8192]{0,1:T(8,128)(2,1)}, bf16[256,8192]{0,1:T(8,128)(2,1)}, u32[]{:S(2)}, u32[]{:S(2)}) %collective-permute-start) | collective-permute-done | bytes 4194336 | tf_op jit(solution)/shard_map/ppermute | solution.py:12
  299.0 6.3 %copy.29 = bf16[1,256,8192]{2,1,0:T(8,128)(2,1)} copy(bf16[1,256,8192]{1,2,0:T(8,128)(2,1)} %bitcast.16) | data formatting | bytes 8388608
  305.3 17.6 %reduce-scatter.2.cloned.1.call-done = f32[12,128,128]{2,1,0:T(8,128)} async-done(((f32[192,128,128]{2,1,0:T(8,128)}), f32[12,128,128]{2,1,0:T(8,128)}) %reduce-scatter.2.cloned.1.call-update) | async-done | bytes 786448 | tf_op jit(solution)/shard_map/reduce_scatter | solution.py:60
  (7 shorter events, 0.0 us)
Async XLA Ops:
  7.2 67.7 %all-gather.5.cloned.1.call-start = ((), (), s32[]{:S(2)}) async-start(), calls=%async_computation.2 | async-start | bytes 6684672 | tf_op jit(solution)/shard_map/all_gather | solution.py:42
  7.9 315.0 %reduce-scatter.2.cloned.1.call-start = ((), (), s32[]{:S(2)}) async-start(), calls=%async_computation.1 | async-start | bytes 13369344 | tf_op jit(solution)/shard_map/reduce_scatter | solution.py:60
  15.6 7.1 %copy-start.3 = (u32[32]{0:T(128)S(1)}, u32[32]{0:T(128)}, u32[]{:S(2)}) copy-start(u32[32]{0:T(128)} %constant.54) | copy-start | bytes 388
  15.6 8.3 %copy-start.1 = (s32[1,12]{1,0:T(1,128)S(1)}, s32[1,12]{1,0:T(1,128)}, u32[]{:S(2)}) copy-start(s32[1,12]{1,0:T(1,128)} %param.13) | copy-start | bytes 148
  15.6 8.4 %copy-start.2 = (s32[1,12]{1,0:T(1,128)S(1)}, s32[1,12]{1,0:T(1,128)}, u32[]{:S(2)}) copy-start(s32[1,12]{1,0:T(1,128)} %param.12) | copy-start | bytes 148
  97.3 56.4 %copy-start = (f32[1,8192]{1,0:T(1,128)S(1)}, f32[1,8192]{1,0:T(1,128)}, u32[]{:S(2)}) copy-start(f32[1,8192]{1,0:T(1,128)} %param.10) | copy-start | bytes 98308
  205.9 93.1 %collective-permute-start = (bf16[256,8192]{0,1:T(8,128)(2,1)}, bf16[256,8192]{0,1:T(8,128)(2,1)}, u32[]{:S(2)}, u32[]{:S(2)}) collective-permute-start(bf16[256,8192]{0,1:T(8,128)(2,1)} %fusion.9), channel_id=1, source_target_pairs={{0,16},{16,0},{1,17},{17,1},{2,18},{18,2},{3,19},{19,3},{4,20},{20... | collective-permute-start | bytes 12582920 | tf_op jit(solution)/shard_map/ppermute | solution.py:12
Sparse Core Ops, SparseCore 0:
  10.3 64.5 all-gather.4
  187.5 135.3 reduce-scatter.1
where the time goes:
time: 331 us; the launch traced here: 330 us
  other arithmetic  78.5 us (24%)
  blocking collectives  76.5 us (23%)
  waiting for transfers between devices  72.1 us (22%)
  local copies, waits for them, and re-layouts  54.4 us (16%)
  matrix products  32 us (10%)
  between operations  14.7 us (4%)
    psum x1, blocking collectives, on_device(): gain_whole = lax.psum(gain_terms, 'fsdp')  62.5 us
    scatter-add x1, other arithmetic, on_device(): start_total.at[:, jnp.where(valid, row_part, 0)].add(product)  56.4 us
    ppermute x1, waiting for transfers between devices, from_behind(): return lax.ppermute(value, axis, pairs)  28.5 us
    all_gather x1, waiting for transfers between devices, on_device(): lax.all_gather(own_tiles, 'fsdp', axis=0, tiled=True)  25.3 us
    dot_general x1, matrix products, on_device(): jnp.einsum('mkj,kij->mki', chosen, lax.all_gather(own_tiles, 'fsdp', axis...  18.1 us
    reduce_scatter x1, waiting for transfers between devices, on_device(): lax.psum_scatter(summed * valid[:, None, None].astype(jnp.float32), 'fsdp...  17.6 us
    unnamed x16, local copies, waits for them, and re-layouts  14.6 us
    all_gather x1, blocking collectives, on_device(): lax.all_gather(tile_rows[0], 'fsdp', axis=0, tiled=True)  13.9 us
  transfers between devices with their start and end apart: 3, of which 3 were waited for; matrix products, arithmetic and copies ran while one was open for 16% of the time, Pallas kernels for 0%

commit v1 on v0

v1 whole, which is shorter than its diff:
```python
import functools

import jax
import jax.numpy as jnp
from jax import lax
from jax.experimental import pallas as pl
from jax.experimental.pallas import tpu as pltpu
from jax.sharding import PartitionSpec as P

EPS = 1e-05
WIDE = 512


def weight_kernel(rows, cols, x_ref, grad_ref, gain_ref, out_ref, dense):
    owner = pl.program_id(0)
    slots, side, _ = out_ref.shape
    width = x_ref.shape[1]

    @pl.when(owner == 0)
    def _():
        def squares(step, total):
            wide = x_ref[:, pl.ds(pl.multiple_of(step * WIDE, WIDE), WIDE)].astype(jnp.float32)
            return total + jnp.sum(wide * wide, axis=-1, keepdims=True)

        total = lax.fori_loop(
            0, width // WIDE, squares, jnp.zeros((x_ref.shape[0], 1), jnp.float32)
        )
        rstd = lax.rsqrt(total / width + EPS)

        def step(i, carry):
            here = pl.ds(pl.multiple_of(i * WIDE, WIDE), WIDE)
            scaled = (x_ref[:, here].astype(jnp.float32) * rstd * gain_ref[:, here]).astype(
                jnp.bfloat16
            )
            dense[here, :] = lax.dot_general(
                scaled, grad_ref[...], (((0,), (0,)), ((), ())), preferred_element_type=jnp.float32
            )
            return carry

        lax.fori_loop(0, width // WIDE, step, 0)

    def pick(slot, carry):
        row = rows[owner * slots + slot]
        col = cols[owner * slots + slot]
        at_row = pl.ds(pl.multiple_of(jnp.maximum(row, 0) * side, side), side)
        at_col = pl.ds(pl.multiple_of(jnp.maximum(col, 0) * side, side), side)
        block = dense[at_row, at_col]
        out_ref[slot] = jnp.where(row >= 0, block, jnp.zeros_like(block))
        return carry

    lax.fori_loop(0, slots, pick, 0)


def weight_sums(x, grads, gain, rows, cols, owners, side):
    tokens, width = x.shape
    slots = rows.shape[0] // owners
    keys = grads.shape[1]
    whole = lambda shape: pl.BlockSpec(shape, lambda i, r, c: (0, 0))
    return pl.pallas_call(
        weight_kernel,
        out_shape=jax.ShapeDtypeStruct((owners * slots, side, side), jnp.float32),
        grid_spec=pltpu.PrefetchScalarGridSpec(
            num_scalar_prefetch=2,
            grid=(owners,),
            in_specs=[whole((tokens, width)), whole((tokens, keys)), whole((1, width))],
            out_specs=pl.BlockSpec((slots, side, side), lambda i, r, c: (i, 0, 0)),
            scratch_shapes=[pltpu.VMEM((width, keys), jnp.float32)],
        ),
        compiler_params=pltpu.CompilerParams(vmem_limit_bytes=40 * 2**20),
        cost_estimate=pl.CostEstimate(
            flops=2 * tokens * width * keys, bytes_accessed=18 * 2**20, transcendentals=0
        ),
        name="weight_sums",
    )(rows, cols, x, grads, gain)


def input_kernel(slot_of, x_ref, grad_ref, gain_ref, tiles_ref, out_ref, dense, feature):
    side = tiles_ref.shape[1]
    tokens, width = x_ref.shape
    keys = grad_ref.shape[1]
    col_blocks = keys // side

    @pl.when(pl.program_id(0) == 0)
    def _():
        def build(row, carry):
            at_row = pl.ds(pl.multiple_of(row * side, side), side)
            for col in range(col_blocks):
                slot = slot_of[row * col_blocks + col]
                block = tiles_ref[jnp.maximum(slot, 0)]
                dense[at_row, col * side : (col + 1) * side] = jnp.where(
                    slot >= 0, block, jnp.zeros_like(block)
                )
            return carry

        lax.fori_loop(0, width // side, build, 0)

    def squares(step, total):
        wide = x_ref[:, pl.ds(pl.multiple_of(step * WIDE, WIDE), WIDE)].astype(jnp.float32)
        return total + jnp.sum(wide * wide, axis=-1, keepdims=True)

    zero = jnp.zeros((tokens, 1), jnp.float32)
    rstd = lax.rsqrt(lax.fori_loop(0, width // WIDE, squares, zero) / width + EPS)

    def product(step, total):
        here = pl.ds(pl.multiple_of(step * WIDE, WIDE), WIDE)
        gained = (
            lax.dot_general(
                grad_ref[...],
                dense[here, :],
                (((1,), (1,)), ((), ())),
                preferred_element_type=jnp.float32,
            )
            * gain_ref[:, here]
        )
        feature[:, here] = gained
        normed = x_ref[:, here].astype(jnp.float32) * rstd
        return total + jnp.sum(gained * normed, axis=-1, keepdims=True)

    mean = lax.fori_loop(0, width // WIDE, product, zero) / width

    def finish(step, carry):
        here = pl.ds(pl.multiple_of(step * WIDE, WIDE), WIDE)
        normed = x_ref[:, here].astype(jnp.float32) * rstd
        out_ref[:, here] = (rstd * (feature[:, here] - normed * mean)).astype(out_ref.dtype)
        return carry

    lax.fori_loop(0, width // WIDE, finish, 0)


def input_part(x, grads, gain, tiles, slot_of):
    tokens, width = x.shape
    keys = grads.shape[1]
    block = min(tokens, 64)
    return pl.pallas_call(
        input_kernel,
        out_shape=jax.ShapeDtypeStruct((tokens, width), jnp.bfloat16),
        grid_spec=pltpu.PrefetchScalarGridSpec(
            num_scalar_prefetch=1,
            grid=(tokens // block,),
            in_specs=[
                pl.BlockSpec((block, width), lambda i, s: (i, 0)),
                pl.BlockSpec((block, keys), lambda i, s: (i, 0)),
                pl.BlockSpec((1, width), lambda i, s: (0, 0)),
                pl.BlockSpec(tiles.shape, lambda i, s: (0, 0, 0)),
            ],
            out_specs=pl.BlockSpec((block, width), lambda i, s: (i, 0)),
            scratch_shapes=[
                pltpu.VMEM((width, keys), jnp.bfloat16),
                pltpu.VMEM((block, width), jnp.float32),
            ],
        ),
        compiler_params=pltpu.CompilerParams(vmem_limit_bytes=40 * 2**20),
        cost_estimate=pl.CostEstimate(
            flops=2 * tokens * width * keys, bytes_accessed=10 * 2**20, transcendentals=0
        ),
        name="input_part",
    )(slot_of, x, grads, gain, tiles)


def reduce_to_owners(sums):
    return lax.psum_scatter(sums, "fsdp", scatter_dimension=0, tiled=True)


def on_device(inputs, out_grad, gain, tiles, tile_rows, tile_cols):
    x, grads, own_tiles = inputs[0], out_grad[0], tiles[0]
    tokens, width = x.shape
    side = own_tiles.shape[-1]
    row_blocks, col_blocks = width // side, grads.shape[1] // side
    owners = lax.axis_size("fsdp")
    sections = lax.axis_size("section")
    section, index = lax.axis_index("section"), lax.axis_index("fsdp")
    behind = [(s, (s - 1) % sections) for s in range(sections)]
    shift = lambda value: lax.ppermute(value, "section", behind)

    next_tiles = shift(own_tiles)
    places = lax.all_gather(
        jnp.concatenate([tile_rows, tile_cols]), ("section", "fsdp"), axis=0, tiled=False
    ).reshape(sections, owners, 2, -1)
    next_places = lax.dynamic_index_in_dim(places, (section + 1) % sections, 0, keepdims=False)
    places = lax.dynamic_index_in_dim(places, section, 0, keepdims=False)
    rows, cols = places[:, 0].reshape(-1), places[:, 1].reshape(-1)
    next_ids = jnp.where(
        next_places[:, 0] >= 0, next_places[:, 0] * col_blocks + next_places[:, 1], -1
    ).reshape(-1)
    all_tiles = lax.all_gather(next_tiles, "fsdp", axis=0, tiled=True)
    hit = next_ids[None, :] == jnp.arange(row_blocks * col_blocks, dtype=jnp.int32)[:, None]
    slot_of = jnp.max(
        jnp.where(hit, jnp.arange(next_ids.shape[0], dtype=jnp.int32)[None, :], -1), axis=1
    )

    next_gain = shift(gain)
    next_grads = shift(grads)
    parts = 4 if tokens % 256 == 0 else 1
    step = tokens // parts
    arrived = []
    behind_of = next_tiles
    for part in range(parts):
        piece, _ = lax.optimization_barrier((x[part * step : (part + 1) * step], behind_of))
        got = shift(piece)
        if part % 2 == 1:
            behind_of = got
        arrived.append(got)

    sums = weight_sums(x, grads, gain, rows, cols, owners, side)
    weight_grad = reduce_to_owners(sums)

    along = jnp.sum(weight_grad * own_tiles.astype(jnp.float32), axis=-1)
    along = lax.all_gather(along, "fsdp", axis=0, tiled=True)
    share = row_blocks // owners
    mine = index * share + jnp.arange(share, dtype=jnp.int32)
    gain_share = jnp.sum(
        jnp.where((rows[None, :] == mine[:, None])[:, :, None], along[None], 0.0), axis=1
    ).reshape(-1)
    gain_share = gain_share / lax.dynamic_slice_in_dim(gain[0], index * share * side, share * side)

    upstream = jnp.concatenate(
        [
            input_part(
                got, next_grads[part * step : (part + 1) * step], next_gain, all_tiles, slot_of
            )
            for part, got in enumerate(arrived)
        ]
    )
    return (weight_grad[None], gain_share[None], upstream[None])


def solution(mesh):
    in_specs = (
        P("section", "fsdp", None),
        P("section", "fsdp", None),
        P("section", None),
        P("section", "fsdp", None, None),
        P("section", "fsdp"),
        P("section", "fsdp"),
    )
    out_specs = (P("section", "fsdp", None, None), P("section", "fsdp"), P("section", "fsdp", None))
    return jax.shard_map(
        on_device, mesh=mesh, in_specs=in_specs, out_specs=out_specs, check_vma=False
    )
```

time: 331 us -> 252 us (0.76)
  other arithmetic: 78.5 us -> 5.36 us
  Pallas kernels: 0 us -> 61.5 us
  local copies, waits for them, and re-layouts: 54.4 us -> 12.7 us
  matrix products: 32 us -> 0 us
  waiting for transfers between devices: 72.1 us -> 86.9 us
  blocking collectives: 76.5 us -> 62.6 us
  starting transfers between devices: 1.5 us -> 8.01 us
    psum x1 -> x0, blocking collectives: 62.5 us -> none  [on_device(): gain_whole = lax.psum(gain_terms, 'fsdp')]
    pallas_call x0 -> x5, Pallas kernels: none -> 61.5 us  [the longest x4 44.2 us: input_part(): pl.pallas_call(input_kernel, out_shape=jax.ShapeDtypeStruct((tokens, widt...]
    scatter-add x1 -> x0, other arithmetic: 56.4 us -> none  [on_device(): start_total.at[:, jnp.where(valid, row_part, 0)].add(product)]
    ppermute x1 -> x7, waiting for transfers between devices: 28.5 us -> 84 us  [on_device(): shift = lambda value: lax.ppermute(value, 'section', behind)]
    all_gather x1 -> x2, blocking collectives: 13.9 us -> 62.6 us  [the longest x1 42.5 us: on_device(): lax.all_gather(jnp.concatenate([tile_rows, tile_cols]), ('section', 'fsdp...]
    dot_general x2 -> x0, matrix products: 32 us -> none  [the longest x1 18.1 us: on_device(): jnp.einsum('mkj,kij->mki', chosen, lax.all_gather(own_tiles, 'fsdp', axis...]
    all_gather x1, waiting for transfers between devices: 25.3 us -> 0.02 us  [on_device(): all_tiles = lax.all_gather(next_tiles, 'fsdp', axis=0, tiled=True)]
    gather x2 -> x0, local copies, waits for them, and re-layouts: 18.4 us -> none  [the longest x1 10.3 us: on_device(): left = jnp.take(scaled_blocks, jnp.where(valid, row_part, 0), axis=1)]
  transfers between devices with their start and end apart: 3 -> 9, of which waited for: 3 -> 4; matrix products, arithmetic and copies ran while one was open for 16% -> 3% of each run, Pallas kernels for 0% -> 24%
where the time goes in v1:
time: 252 us; the launch traced here: 251 us
  waiting for transfers between devices  86.9 us (34%)
  blocking collectives  62.6 us (25%)
  Pallas kernels  61.5 us (24%)
  between operations  14.2 us (6%)
  local copies, waits for them, and re-layouts  12.7 us (5%)
  starting transfers between devices  8.01 us (3%)
  other arithmetic  5.36 us (2%)
    ppermute x7, waiting for transfers between devices, on_device(): shift = lambda value: lax.ppermute(value, 'section', behind)  84 us
    pallas_call x4, Pallas kernels, input_part(): pl.pallas_call(input_kernel, out_shape=jax.ShapeDtypeStruct((tokens, widt...  44.2 us
    all_gather x1, blocking collectives, on_device(): lax.all_gather(jnp.concatenate([tile_rows, tile_cols]), ('section', 'fsdp...  42.5 us
    all_gather x1, blocking collectives, on_device(): along = lax.all_gather(along, 'fsdp', axis=0, tiled=True)  20.1 us
    pallas_call x1, Pallas kernels, weight_sums(): pl.pallas_call(weight_kernel, out_shape=jax.ShapeDtypeStruct((owners * sl...  17.3 us
    ppermute x7, starting transfers between devices, on_device(): shift = lambda value: lax.ppermute(value, 'section', behind)  7.94 us
    unnamed x17, local copies, waits for them, and re-layouts  7.45 us
  transfers between devices with their start and end apart: 9, of which 4 were waited for; matrix products, arithmetic and copies ran while one was open for 3% of the time, Pallas kernels for 24%

profile of v1, /device:TPU:0, one launch (start us, length us, event | category | flops | bytes accessed | tf_op | source)
XLA Modules:
  0.0 251.1 jit_solution(4637963560750072104)
XLA Ops:
  7.2 0.0 all-gather.5.cloned.1.call-start
  7.2 3.0 %collective-permute-start = (bf16[12,128,128]{2,1,0:T(8,128)(2,1)}, bf16[12,128,128]{2,1,0:T(8,128)(2,1)S(1)}, u32[]{:S(2)}, u32[]{:S(2)}) collective-permute-start(bf16[12,128,128]{2,1,0:T(8,128)(2,1)} %bitcast.34), channel_id=1, source_target_pairs={{0,16},{16,0},{1,17},{17,1},{2,18},{18,2},{3,19},{19,3},{4,20},{20... | collective-permute-start | bytes 1179656 | tf_op jit(solution)/shard_map/ppermute | solution.py:173
  10.2 9.3 %collective-permute-done = bf16[12,128,128]{2,1,0:T(8,128)(2,1)S(1)} collective-permute-done((bf16[12,128,128]{2,1,0:T(8,128)(2,1)}, bf16[12,128,128]{2,1,0:T(8,128)(2,1)S(1)}, u32[]{:S(2)}, u32[]{:S(2)}) %collective-permute-start) | collective-permute-done | bytes 393248 | tf_op jit(solution)/shard_map/ppermute | solution.py:173
  19.5 0.0 copy-start.7
  19.5 0.8 copy-done.7
  20.3 0.0 all-gather.5.cloned.1.call-update
  20.3 0.0 reduce-scatter.2.cloned.1.call-start
  20.4 0.7 add_bitcast_fusion
  21.1 42.5 %all-gather.1 = s32[32,2,12]{2,1,0:T(2,128)S(1)} all-gather(s32[1,2,12]{2,1,0:T(2,128)S(1)} %add_bitcast_fusion), channel_id=2, replica_groups=mesh['section'=2,'fsdp'=16] {'section','fsdp'}, dimensions={0}, use_global_device_ids=true | all-gather | bytes 3168 | tf_op jit(solution)/shard_map/all_gather | solution.py:176
  63.6 0.1 reshape_squeeze.6.rows
  63.6 0.1 reshape_squeeze.7.cols
  63.7 0.0 copy-start.2
  63.7 2.2 copy-done.2
  65.9 0.0 copy-start.3
  65.9 0.9 copy-done.3
  66.9 0.0 copy-start.5
  66.9 0.8 copy-done.5
  67.6 17.3 %weight_sums.1 = f32[192,128,128]{2,1,0:T(8,128)} custom-call(s32[192]{0:T(256)S(1)} %reshape_squeeze.6.rows, s32[192]{0:T(256)S(1)} %reshape_squeeze.7.cols, bf16[256,8192]{1,0:T(8,128)(2,1)S(1)} %bitcast.30, bf16[256,512]{1,0:T(8,128)(2,1)S(1)} %bitcast.31, f32[1,8192]{1,0:T(1,128)S(1)} %copy-done.5), custom_call_target="tpu_custom_call" | custom-call | flops 2147483648 | bytes 18874368 | tf_op jit(solution)/shard_map/weight_sums/pallas_call | solution.py:59
  84.9 0.0 reduce-scatter.2.cloned.1.call-update
  85.0 0.0 copy-start.4
  85.0 0.0 copy-start.6
  85.0 3.9 %slice_bitcast_fusion.3 = (bf16[64,8192]{1,0:T(8,128)(2,1)}, bf16[64,8192]{1,0:T(8,128)(2,1)S(1)}, bf16[64,8192]{1,0:T(8,128)(2,1)}, bf16[64,8192]{1,0:T(8,128)(2,1)}) fusion(bf16[1,256,8192]{2,1,0:T(8,128)(2,1)} %param.6), kind=kLoop, calls=%fused_computation.4 | loop fusion | bytes 8388608 | tf_op jit(solution)/shard_map/slice | solution.py:198
  88.9 0.5 collective-permute-start.4
  89.4 24.9 %collective-permute-done.4.x_ref = bf16[64,8192]{1,0:T(8,128)(2,1)S(1)} collective-permute-done((bf16[64,8192]{1,0:T(8,128)(2,1)S(1)}, bf16[64,8192]{1,0:T(8,128)(2,1)S(1)}, u32[]{:S(2)}, u32[]{:S(2)}) %collective-permute-start.4) | collective-permute-done | bytes 1048608 | tf_op jit(solution)/shard_map/ppermute | solution.py:173
  114.3 0.4 collective-permute-start.6
  114.7 1.6 collective-permute-start.5
  116.3 0.0 copy-done.4
  116.3 0.4 collective-permute-start.2
  116.8 0.0 copy-done.6
  116.8 1.6 collective-permute-start.3
  118.4 0.4 collective-permute-start.1
  118.8 0.1 select_n.42
  118.9 0.1 select_reduce_fusion.1.slot_of
  119.0 0.1 broadcast_compare_fusion
  119.1 49.7 %collective-permute-done.2 = bf16[256,512]{1,0:T(8,128)(2,1)} collective-permute-done((bf16[256,512]{1,0:T(8,128)(2,1)S(1)}, bf16[256,512]{1,0:T(8,128)(2,1)}, u32[]{:S(2)}, u32[]{:S(2)}) %collective-permute-start.2) | collective-permute-done | bytes 262176 | tf_op jit(solution)/shard_map/ppermute | solution.py:173
  168.8 1.0 fusion.1
  169.8 0.0 collective-permute-done.3.gain_ref
  169.8 0.0 all-gather.5.cloned.1.call-done.tiles_ref
  169.8 0.0 copy-start
  169.8 2.8 %copy-done = bf16[192,128,128]{2,1,0:T(8,128)(2,1)S(1)} copy-done((bf16[192,128,128]{2,1,0:T(8,128)(2,1)S(1)}, bf16[192,128,128]{2,1,0:T(8,128)(2,1)}, u32[]{:S(2)}) %copy-start) | copy-done | bytes 6291480
  172.6 0.0 copy-start.1
  172.6 10.7 %input_part.5 = bf16[64,8192]{1,0:T(8,128)(2,1)S(1)} custom-call(s32[256]{0:T(256)S(1)} %select_reduce_fusion.1.slot_of, bf16[64,8192]{1,0:T(8,128)(2,1)S(1)} %collective-permute-done.4.x_ref, bf16[64,512]{1,0:T(8,128)(2,1)S(1)} %get-tuple-element.18.grad_ref, f32[1,8192]{1,0:T(1,128)S(1)} %collective-permute-done.3.gain_ref, bf16[192,128,128]{2,1,0:T(8,128)(2,1)S(1)} %copy-done), custom_call_target="tpu_custom_call" | custom-call | flops 536870912 | bytes 10485760 | tf_op jit(solution)/shard_map/input_part/pallas_call | solution.py:134
  183.3 0.0 collective-permute-done.6.x_ref
  183.4 0.0 copy-done.1
  183.4 10.7 %input_part.7 = bf16[64,8192]{1,0:T(8,128)(2,1)S(1)} custom-call(s32[256]{0:T(256)S(1)} %select_reduce_fusion.1.slot_of, bf16[64,8192]{1,0:T(8,128)(2,1)S(1)} %collective-permute-done.6.x_ref, bf16[64,512]{1,0:T(8,128)(2,1)S(1)} %get-tuple-element.16.grad_ref, f32[1,8192]{1,0:T(1,128)S(1)} %collective-permute-done.3.gain_ref, ...), custom_call_target="tpu_custom_call" | custom-call | flops 536870912 | bytes 10485760 | tf_op jit(solution)/shard_map/input_part/pallas_call | solution.py:134
  194.1 0.0 collective-permute-done.5.x_ref
  194.1 10.7 %input_part.6 = bf16[64,8192]{1,0:T(8,128)(2,1)S(1)} custom-call(s32[256]{0:T(256)S(1)} %select_reduce_fusion.1.slot_of, bf16[64,8192]{1,0:T(8,128)(2,1)S(1)} %collective-permute-done.5.x_ref, bf16[64,512]{1,0:T(8,128)(2,1)S(1)} %get-tuple-element.17.grad_ref, f32[1,8192]{1,0:T(1,128)S(1)} %collective-permute-done.3.gain_ref, ...), custom_call_target="tpu_custom_call" | custom-call | flops 536870912 | bytes 10485760 | tf_op jit(solution)/shard_map/input_part/pallas_call | solution.py:134
  204.9 0.0 collective-permute-done.1.x_ref
  204.9 12.0 %input_part.4 = bf16[64,8192]{1,0:T(8,128)(2,1)S(1)} custom-call(s32[256]{0:T(256)S(1)} %select_reduce_fusion.1.slot_of, bf16[64,8192]{1,0:T(8,128)(2,1)} %collective-permute-done.1.x_ref, bf16[64,512]{1,0:T(8,128)(2,1)S(1)} %get-tuple-element.15.grad_ref, f32[1,8192]{1,0:T(1,128)S(1)} %collective-permute-done.3.gain_ref, bf16[192,128,128]{2,1,0:T(8,128)(2,1)S(1)} %copy-done.1), custom_call_target="tpu_custom_call" | custom-call | flops 536870912 | bytes 10485760 | tf_op jit(solution)/shard_map/input_part/pallas_call | solution.py:134
  216.8 2.2 maximum_bitcast_fusion
  219.0 2.8 %reduce-scatter.2.cloned.1.call-done = f32[12,128,128]{2,1,0:T(8,128)} async-done(((f32[192,128,128]{2,1,0:T(8,128)}), f32[12,128,128]{2,1,0:T(8,128)}) %reduce-scatter.2.cloned.1.call-update) | async-done | bytes 786448 | tf_op jit(solution)/shard_map/reduce_scatter | solution.py:161
  221.9 1.5 multiply_reduce_fusion
  223.4 20.1 %all-gather.2 = f32[16,12,128]{2,1,0:T(8,128)S(1)} all-gather(f32[1,12,128]{2,1,0:T(8,128)S(1)} %bitcast.36), channel_id=1, replica_groups=mesh['section'=2,'fsdp'=16] {'fsdp'}, dimensions={0}, use_global_device_ids=true | all-gather | bytes 104448 | tf_op jit(solution)/shard_map/all_gather | solution.py:208
  243.5 0.2 select_reduce_fusion
  243.7 0.6 dynamic-slice_divide_fusion
  (6 shorter events, 0.0 us)
Async XLA Ops:
  7.2 162.7 %all-gather.5.cloned.1.call-start = ((), (), s32[]{:S(2)}) async-start(), calls=%async_computation.2 | async-start | bytes 6684672 | tf_op jit(solution)/shard_map/all_gather | solution.py:185
  7.2 12.3 %collective-permute-start = (bf16[12,128,128]{2,1,0:T(8,128)(2,1)}, bf16[12,128,128]{2,1,0:T(8,128)(2,1)S(1)}, u32[]{:S(2)}, u32[]{:S(2)}) collective-permute-start(bf16[12,128,128]{2,1,0:T(8,128)(2,1)} %bitcast.34), channel_id=1, source_target_pairs={{0,16},{16,0},{1,17},{17,1},{2,18},{18,2},{3,19},{19,3},{4,20},{20... | collective-permute-start | bytes 1179656 | tf_op jit(solution)/shard_map/ppermute | solution.py:173
  19.5 0.8 copy-start.7
  20.3 201.5 %reduce-scatter.2.cloned.1.call-start = ((), (), s32[]{:S(2)}) async-start(), calls=%async_computation.1 | async-start | bytes 13369344 | tf_op jit(solution)/shard_map/reduce_scatter | solution.py:161
  63.7 2.2 copy-start.2
  65.9 0.9 copy-start.3
  66.9 0.8 copy-start.5
  85.0 31.4 %copy-start.4 = (bf16[1,256,512]{2,1,0:T(8,128)(2,1)S(1)}, bf16[1,256,512]{2,1,0:T(8,128)(2,1)}, u32[]{:S(2)}) copy-start(bf16[1,256,512]{2,1,0:T(8,128)(2,1)} %param.7) | copy-start | bytes 786436
  85.0 31.8 %copy-start.6 = (f32[1,8192]{1,0:T(1,128)S(1)}, f32[1,8192]{1,0:T(1,128)}, u32[]{:S(2)}) copy-start(f32[1,8192]{1,0:T(1,128)} %gain_ref.1) | copy-start | bytes 98308
  88.9 25.4 %collective-permute-start.4 = (bf16[64,8192]{1,0:T(8,128)(2,1)S(1)}, bf16[64,8192]{1,0:T(8,128)(2,1)S(1)}, u32[]{:S(2)}, u32[]{:S(2)}) collective-permute-start(bf16[64,8192]{1,0:T(8,128)(2,1)S(1)} %get-tuple-element.8), channel_id=1, source_target_pairs={{0,16},{16,0},{1,17},{17,1},{2,18},{18,2},{3,19},{19,3},{4,20},{20... | collective-permute-start | bytes 3145736 | tf_op jit(solution)/shard_map/ppermute | solution.py:173
  114.3 69.0 %collective-permute-start.6 = (bf16[64,8192]{1,0:T(8,128)(2,1)}, bf16[64,8192]{1,0:T(8,128)(2,1)S(1)}, u32[]{:S(2)}, u32[]{:S(2)}) collective-permute-start(bf16[64,8192]{1,0:T(8,128)(2,1)} %get-tuple-element.10), channel_id=1, source_target_pairs={{0,16},{16,0},{1,17},{17,1},{2,18},{18,2},{3,19},{19,3},{4,20},{20... | collective-permute-start | bytes 3145736 | tf_op jit(solution)/shard_map/ppermute | solution.py:173
  114.7 79.4 %collective-permute-start.5 = (bf16[64,8192]{1,0:T(8,128)(2,1)}, bf16[64,8192]{1,0:T(8,128)(2,1)S(1)}, u32[]{:S(2)}, u32[]{:S(2)}) collective-permute-start(bf16[64,8192]{1,0:T(8,128)(2,1)} %get-tuple-element.9), channel_id=1, source_target_pairs={{0,16},{16,0},{1,17},{17,1},{2,18},{18,2},{3,19},{19,3},{4,20},{20... | collective-permute-start | bytes 3145736 | tf_op jit(solution)/shard_map/ppermute | solution.py:173
  116.3 52.5 %collective-permute-start.2 = (bf16[256,512]{1,0:T(8,128)(2,1)S(1)}, bf16[256,512]{1,0:T(8,128)(2,1)}, u32[]{:S(2)}, u32[]{:S(2)}) collective-permute-start(bf16[256,512]{1,0:T(8,128)(2,1)S(1)} %bitcast.32), channel_id=1, source_target_pairs={{0,16},{16,0},{1,17},{17,1},{2,18},{18,2},{3,19},{19,3},{4,20},{20... | collective-permute-start | bytes 786440 | tf_op jit(solution)/shard_map/ppermute | solution.py:173
  116.8 53.0 %collective-permute-start.3 = (f32[1,8192]{1,0:T(1,128)S(1)}, f32[1,8192]{1,0:T(1,128)S(1)}, u32[]{:S(2)}, u32[]{:S(2)}) collective-permute-start(f32[1,8192]{1,0:T(1,128)S(1)} %copy-done.6), channel_id=1, source_target_pairs={{0,16},{16,0},{1,17},{17,1},{2,18},{18,2},{3,19},{19,3},{4,20},{20... | collective-permute-start | bytes 98312 | tf_op jit(solution)/shard_map/ppermute | solution.py:173
  118.4 86.5 %collective-permute-start.1 = (bf16[64,8192]{1,0:T(8,128)(2,1)}, bf16[64,8192]{1,0:T(8,128)(2,1)}, u32[]{:S(2)}, u32[]{:S(2)}) collective-permute-start(bf16[64,8192]{1,0:T(8,128)(2,1)} %get-tuple-element.7), channel_id=1, source_target_pairs={{0,16},{16,0},{1,17},{17,1},{2,18},{18,2},{3,19},{19,3},{4,20},{20... | collective-permute-start | bytes 3145736 | tf_op jit(solution)/shard_map/ppermute | solution.py:173
  169.8 2.8 %copy-start = (bf16[192,128,128]{2,1,0:T(8,128)(2,1)S(1)}, bf16[192,128,128]{2,1,0:T(8,128)(2,1)}, u32[]{:S(2)}) copy-start(bf16[192,128,128]{2,1,0:T(8,128)(2,1)} %all-gather.5.cloned.1.call-done.tiles_ref) | copy-start | bytes 18874372
  172.6 10.7 %copy-start.1 = (bf16[192,128,128]{2,1,0:T(8,128)(2,1)S(1)}, bf16[192,128,128]{2,1,0:T(8,128)(2,1)}, u32[]{:S(2)}) copy-start(bf16[192,128,128]{2,1,0:T(8,128)(2,1)} %all-gather.5.cloned.1.call-done.tiles_ref) | copy-start | bytes 18874372
Sparse Core Ops, SparseCore 0:
  20.4 63.4 all-gather.4
  88.6 133.2 reduce-scatter.1

commit v2 on v1

--- a/solution.py
+++ b/solution.py
@@ -74,25 +74,42 @@
     )(rows, cols, x, grads, gain)
 
 
-def input_kernel(slot_of, x_ref, grad_ref, gain_ref, tiles_ref, out_ref, dense, feature):
+def dense_kernel(slot_of, tiles_ref, out_ref):
     side = tiles_ref.shape[1]
+    first = pl.program_id(0) * (out_ref.shape[0] // side)
+    col_blocks = out_ref.shape[1] // side
+
+    def build(row, carry):
+        at_row = pl.ds(pl.multiple_of(row * side, side), side)
+        for col in range(col_blocks):
+            slot = slot_of[(first + row) * col_blocks + col]
+            block = tiles_ref[jnp.maximum(slot, 0)]
+            out_ref[at_row, col * side : (col + 1) * side] = jnp.where(
+                slot >= 0, block, jnp.zeros_like(block)
+            )
+        return carry
+
+    lax.fori_loop(0, out_ref.shape[0] // side, build, 0)
+
+
+def dense_weights(tiles, slot_of, width, keys):
+    return pl.pallas_call(
+        dense_kernel,
+        out_shape=jax.ShapeDtypeStruct((width, keys), tiles.dtype),
+        grid_spec=pltpu.PrefetchScalarGridSpec(
+            num_scalar_prefetch=1,
+            grid=(8,),
+            in_specs=[pl.BlockSpec(tiles.shape, lambda i, s: (0, 0, 0))],
+            out_specs=pl.BlockSpec((width // 8, keys), lambda i, s: (i, 0)),
+        ),
+        compiler_params=pltpu.CompilerParams(vmem_limit_bytes=40 * 2**20),
+        cost_estimate=pl.CostEstimate(flops=0, bytes_accessed=15 * 2**20, transcendentals=0),
+        name="dense_weights",
+    )(slot_of, tiles)
+
+
+def input_kernel(x_ref, grad_ref, gain_ref, dense, out_ref, feature):
     tokens, width = x_ref.shape
-    keys = grad_ref.shape[1]
-    col_blocks = keys // side
-
-    @pl.when(pl.program_id(0) == 0)
-    def _():
-        def build(row, carry):
-            at_row = pl.ds(pl.multiple_of(row * side, side), side)
-            for col in range(col_blocks):
-                slot = slot_of[row * col_blocks + col]
-                block = tiles_ref[jnp.maximum(slot, 0)]
-                dense[at_row, col * side : (col + 1) * side] = jnp.where(
-                    slot >= 0, block, jnp.zeros_like(block)
-                )
-            return carry
-
-        lax.fori_loop(0, width // side, build, 0)
 
     def squares(step, total):
         wide = x_ref[:, pl.ds(pl.multiple_of(step * WIDE, WIDE), WIDE)].astype(jnp.float32)
@@ -127,38 +144,201 @@
     lax.fori_loop(0, width // WIDE, finish, 0)
 
 
-def input_part(x, grads, gain, tiles, slot_of):
+def input_part(x, grads, gain, dense):
     tokens, width = x.shape
     keys = grads.shape[1]
     block = min(tokens, 64)
     return pl.pallas_call(
         input_kernel,
         out_shape=jax.ShapeDtypeStruct((tokens, width), jnp.bfloat16),
-        grid_spec=pltpu.PrefetchScalarGridSpec(
-            num_scalar_prefetch=1,
-            grid=(tokens // block,),
-            in_specs=[
-                pl.BlockSpec((block, width), lambda i, s: (i, 0)),
-                pl.BlockSpec((block, keys), lambda i, s: (i, 0)),
-                pl.BlockSpec((1, width), lambda i, s: (0, 0)),
-                pl.BlockSpec(tiles.shape, lambda i, s: (0, 0, 0)),
-            ],
-            out_specs=pl.BlockSpec((block, width), lambda i, s: (i, 0)),
-            scratch_shapes=[
-                pltpu.VMEM((width, keys), jnp.bfloat16),
-                pltpu.VMEM((block, width), jnp.float32),
-            ],
-        ),
+        grid=(tokens // block,),
+        in_specs=[
+            pl.BlockSpec((block, width), lambda i: (i, 0)),
+            pl.BlockSpec((block, keys), lambda i: (i, 0)),
+            pl.BlockSpec((1, width), lambda i: (0, 0)),
+            pl.BlockSpec(dense.shape, lambda i: (0, 0)),
+        ],
+        out_specs=pl.BlockSpec((block, width), lambda i: (i, 0)),
+        scratch_shapes=[pltpu.VMEM((block, width), jnp.float32)],
         compiler_params=pltpu.CompilerParams(vmem_limit_bytes=40 * 2**20),
         cost_estimate=pl.CostEstimate(
             flops=2 * tokens * width * keys, bytes_accessed=10 * 2**20, transcendentals=0
         ),
         name="input_part",
-    )(slot_of, x, grads, gain, tiles)
+    )(x, grads, gain, dense)
+
+
+def owner_kernel(lines, levels, sums, out_ref, half, near, stage, across, up, down, load, sems):
+    index = lax.axis_index("fsdp")
+    core, line, level = index % 2, (index // 2) % lines, index // (2 * lines)
+    place = lambda at_level, at_line, at_core: (at_level * lines + at_line) * 2 + at_core
+    near_send, near_recv, across_send, across_recv, up_send, up_recv, down_send, down_recv = sems
+
+    def copy(source, target, send, recv, device):
+        return pltpu.make_async_remote_copy(
+            src_ref=source,
+            dst_ref=target,
+            send_sem=send,
+            recv_sem=recv,
+            device_id={"fsdp": device},
+            device_id_type=pl.DeviceIdType.MESH,
+        )
+
+    barrier = pltpu.get_barrier_semaphore()
+    greet = lambda device: pl.semaphore_signal(
+        barrier, inc=1, device_id={"fsdp": device}, device_id_type=pl.DeviceIdType.MESH
+    )
+    greet(place(level, line, 1 - core))
+    for ahead in range(1, lines):
+        greet(place(level, (line + ahead) % lines, core))
+    pl.when(level > 0)(lambda: greet(place(level - 1, line, core)))
+    pl.when(level < levels - 1)(lambda: greet(place(level + 1, line, core)))
+    below = (level + levels - 1) // levels
+    above = (2 * (levels - 1) - level) // levels
+    pl.semaphore_wait(barrier, lines + below + above)
+
+    middle = levels // 2
+    upper = level // middle
+    order = []
+    for k in range(levels):
+        low = levels - 1 - k if k < middle else k - middle
+        high = k if k < middle else levels - 1 - k + middle
+        order.append((1 - upper) * low + upper * high)
+
+    def to_core(t, y):
+        return copy(
+            sums.at[place(t, y, 1 - core)],
+            near.at[t, y],
+            near_send.at[t, y],
+            near_recv.at[t, y],
+            place(level, line, 1 - core),
+        )
+
+    def own(t, y):
+        return pltpu.make_async_copy(sums.at[place(t, y, core)], half.at[t, y], load.at[t, y])
+
+    def to_line(t, ahead):
+        return copy(
+            stage.at[ahead - 1, t],
+            across.at[ahead - 1, t],
+            across_send.at[ahead - 1, t],
+            across_recv.at[ahead - 1, t],
+            place(level, (line + ahead) % lines, core),
+        )
+
+    def to_up(t):
+        return copy(
+            half.at[t, line], up.at[t], up_send.at[t], up_recv.at[t], place(level + 1, line, core)
+        )
+
+    def to_down(t):
+        return copy(
+            half.at[t, line],
+            down.at[t],
+            down_send.at[t],
+            down_recv.at[t],
+            place(level - 1, line, core),
+        )
+
+    for t in order:
+        for y in range(lines):
+            to_core(t, y).start()
+            own(t, y).start()
+    for t in order:
+        for y in range(lines):
+            own(t, y).wait()
+            to_core(t, y).wait_recv()
+        for ahead in range(1, lines):
+            y = (line + ahead) % lines
+            stage[ahead - 1, t] = (half[t, y] + near[t, y]).astype(jnp.bfloat16)
+            to_line(t, ahead).start()
+    for t in order:
+        total = half[t, line] + near[t, line]
+        for ahead in range(1, lines):
+            to_line(t, ahead).wait_recv()
+            total = total + across[ahead - 1, t].astype(jnp.float32)
+        half[t, line] = total
+
+        @pl.when(level < t)
+        def _():
+            @pl.when(level > 0)
+            def _():
+                to_up(t).wait_recv()
+                half[t, line] += up[t]
+
+            to_up(t).start()
+
+        @pl.when(level > t)
+        def _():
+            @pl.when(level < levels - 1)
+            def _():
+                to_down(t).wait_recv()
+                half[t, line] += down[t]
+
+            to_down(t).start()
+
+    out_ref[...] = half[level, line]
+
+    @pl.when(level > 0)
+    def _():
+        to_up(level).wait_recv()
+        out_ref[...] += up[level]
+
+    @pl.when(level < levels - 1)
+    def _():
+        to_down(level).wait_recv()
+        out_ref[...] += down[level]
+
+    for t in order:
+        for y in range(lines):
+            to_core(t, y).wait_send()
+        for ahead in range(1, lines):
+            to_line(t, ahead).wait_send()
+        pl.when(level < t)(lambda: to_up(t).wait_send())
+        pl.when(level > t)(lambda: to_down(t).wait_send())
 
 
 def reduce_to_owners(sums):
-    return lax.psum_scatter(sums, "fsdp", scatter_dimension=0, tiled=True)
+    owners = lax.axis_size("fsdp")
+    lines = 2
+    while lines * lines * 4 <= owners // 2:
+        lines *= 2
+    levels = owners // 2 // lines
+    slots, side = sums.shape[0] // owners, sums.shape[1]
+    block = (slots, side, side)
+    dma = lambda *shape: pltpu.SemaphoreType.DMA(shape)
+    return pl.pallas_call(
+        functools.partial(owner_kernel, lines, levels),
+        out_shape=jax.ShapeDtypeStruct(block, jnp.float32),
+        in_specs=[pl.BlockSpec(memory_space=pl.ANY)],
+        out_specs=pl.BlockSpec(memory_space=pltpu.VMEM),
+        scratch_shapes=[
+            pltpu.VMEM((levels, lines) + block, jnp.float32),
+            pltpu.VMEM((levels, lines) + block, jnp.float32),
+            pltpu.VMEM((lines - 1, levels) + block, jnp.bfloat16),
+            pltpu.VMEM((lines - 1, levels) + block, jnp.bfloat16),
+            pltpu.VMEM((levels,) + block, jnp.float32),
+            pltpu.VMEM((levels,) + block, jnp.float32),
+            dma(levels, lines),
+            [
+                dma(levels, lines),
+                dma(levels, lines),
+                dma(lines - 1, levels),
+                dma(lines - 1, levels),
+                dma(levels),
+                dma(levels),
+                dma(levels),
+                dma(levels),
+            ],
+        ],
+        compiler_params=pltpu.CompilerParams(
+            collective_id=0, has_side_effects=True, vmem_limit_bytes=40 * 2**20
+        ),
+        cost_estimate=pl.CostEstimate(
+            flops=10**7, bytes_accessed=250 * 2**20, transcendentals=0
+        ),
+        name="owner_sums",
+    )(sums.reshape((owners,) + block))
 
 
 def on_device(inputs, out_grad, gain, tiles, tile_rows, tile_cols):
@@ -182,6 +362,7 @@
     next_ids = jnp.where(
         next_places[:, 0] >= 0, next_places[:, 0] * col_blocks + next_places[:, 1], -1
     ).reshape(-1)
+    next_tiles, next_ids = lax.optimization_barrier((next_tiles, next_ids))
     all_tiles = lax.all_gather(next_tiles, "fsdp", axis=0, tiled=True)
     hit = next_ids[None, :] == jnp.arange(row_blocks * col_blocks, dtype=jnp.int32)[:, None]
     slot_of = jnp.max(
@@ -193,15 +374,12 @@
     parts = 4 if tokens % 256 == 0 else 1
     step = tokens // parts
     arrived = []
-    behind_of = next_tiles
+    x_later, _ = lax.optimization_barrier((x, next_tiles))
     for part in range(parts):
-        piece, _ = lax.optimization_barrier((x[part * step : (part + 1) * step], behind_of))
-        got = shift(piece)
-        if part % 2 == 1:
-            behind_of = got
-        arrived.append(got)
-
-    sums = weight_sums(x, grads, gain, rows, cols, owners, side)
+        arrived.append(shift(x_later[part * step : (part + 1) * step]))
+
+    x_first, _ = lax.optimization_barrier((x, next_tiles))
+    sums = weight_sums(x_first, grads, gain, rows, cols, owners, side)
     weight_grad = reduce_to_owners(sums)
 
     along = jnp.sum(weight_grad * own_tiles.astype(jnp.float32), axis=-1)
@@ -213,11 +391,10 @@
     ).reshape(-1)
     gain_share = gain_share / lax.dynamic_slice_in_dim(gain[0], index * share * side, share * side)
 
+    dense = dense_weights(all_tiles, slot_of, width, grads.shape[1])
     upstream = jnp.concatenate(
         [
-            input_part(
-                got, next_grads[part * step : (part + 1) * step], next_gain, all_tiles, slot_of
-            )
+            input_part(got, next_grads[part * step : (part + 1) * step], next_gain, dense)
             for part, got in enumerate(arrived)
         ]
     )

time: 252 us -> 247 us (0.980)
  waiting for transfers between devices: 86.9 us -> 0.36 us
  Pallas kernels: 61.5 us -> 141 us
  local copies, waits for them, and re-layouts: 12.7 us -> 17.2 us
    pallas_call x0 -> x2, Pallas kernels: none -> 89.7 us  [the longest x1 83.6 us: reduce_to_owners(): pl.pallas_call(functools.partial(owner_kernel, lines, levels), out_shape=...]
    ppermute x7, waiting for transfers between devices: 84 us -> 0.33 us  [on_device(): shift = lambda value: lax.ppermute(value, 'section', behind)]
    pallas_call x4, Pallas kernels: 44.2 us -> 33.6 us  [input_part(): pl.pallas_call(input_kernel, out_shape=jax.ShapeDtypeStruct((tokens, widt...]
    unnamed x17 -> x18, local copies, waits for them, and re-layouts: 7.45 us -> 12.4 us
    reduce_scatter x1 -> x0, waiting for transfers between devices: 2.83 us -> none  [reduce_to_owners(): return lax.psum_scatter(sums, 'fsdp', scatter_dimension=0, tiled=True)]
  transfers between devices with their start and end apart: 9 -> 8, of which waited for: 4 -> 1; matrix products, arithmetic and copies ran while one was open for 3% -> 3% of each run, Pallas kernels for 24% -> 54%
where the time goes in v2:
time: 247 us
  Pallas kernels  141 us (57%)
  blocking collectives  61.4 us (25%)
  local copies, waits for them, and re-layouts  17.2 us (7%)
  between operations  14.2 us (6%)
  starting transfers between devices  9.06 us (4%)
  other arithmetic  4.18 us (2%)
    pallas_call x1, Pallas kernels, reduce_to_owners(): pl.pallas_call(functools.partial(owner_kernel, lines, levels), out_shape=...  83.6 us
    all_gather x1, blocking collectives, on_device(): lax.all_gather(jnp.concatenate([tile_rows, tile_cols]), ('section', 'fsdp...  40.8 us
    pallas_call x4, Pallas kernels, input_part(): pl.pallas_call(input_kernel, out_shape=jax.ShapeDtypeStruct((tokens, widt...  33.6 us
    all_gather x1, blocking collectives, on_device(): along = lax.all_gather(along, 'fsdp', axis=0, tiled=True)  20.6 us
    pallas_call x1, Pallas kernels, weight_sums(): pl.pallas_call(weight_kernel, out_shape=jax.ShapeDtypeStruct((owners * sl...  17.3 us
    unnamed x18, local copies, waits for them, and re-layouts  12.4 us
    ppermute x7, starting transfers between devices, on_device(): shift = lambda value: lax.ppermute(value, 'section', behind)  9.02 us
    pallas_call x1, Pallas kernels, dense_weights(): pl.pallas_call(dense_kernel, out_shape=jax.ShapeDtypeStruct((width, keys)...  6.1 us
  transfers between devices with their start and end apart: 8, of which 1 were waited for; matrix products, arithmetic and copies ran while one was open for 3% of the time, Pallas kernels for 54%

profile of v2, /device:TPU:0, one launch (start us, length us, event | category | flops | bytes accessed | tf_op | source)
XLA Modules:
  0.0 247.0 jit_solution(3021485088368019385)
XLA Ops:
  7.2 0.0 copy-start.5
  7.2 0.0 copy-start.4
  7.2 0.0 all-gather.5.cloned.1.call-start
  7.2 3.0 %collective-permute-start = (bf16[12,128,128]{2,1,0:T(8,128)(2,1)}, bf16[12,128,128]{2,1,0:T(8,128)(2,1)S(1)}, u32[]{:S(2)}, u32[]{:S(2)}) collective-permute-start(bf16[12,128,128]{2,1,0:T(8,128)(2,1)} %bitcast.29), channel_id=1, source_target_pairs={{0,16},{16,0},{1,17},{17,1},{2,18},{18,2},{3,19},{19,3},{4,20},{20... | collective-permute-start | bytes 1179656 | tf_op jit(solution)/shard_map/ppermute | solution.py:353
  10.2 0.7 add_bitcast_fusion
  10.9 40.8 %all-gather.1 = s32[32,2,12]{2,1,0:T(2,128)S(1)} all-gather(s32[1,2,12]{2,1,0:T(2,128)S(1)} %add_bitcast_fusion), channel_id=2, replica_groups=mesh['section'=2,'fsdp'=16] {'section','fsdp'}, dimensions={0}, use_global_device_ids=true | all-gather | bytes 3168 | tf_op jit(solution)/shard_map/all_gather | solution.py:356
  51.8 0.1 select_n.37
  51.9 0.0 collective-permute-done
  51.9 0.0 copy-start.6
  51.9 0.7 copy-done.6
  52.6 0.0 all-gather.5.cloned.1.call-update
  52.7 1.6 collective-permute-start.3
  54.2 0.5 collective-permute-start.2
  54.7 0.1 reshape_squeeze.7.cols
  54.8 0.1 reshape_squeeze.6.rows
  54.9 0.0 copy-start.2
  54.9 0.1 broadcast_compare_fusion
  55.0 4.5 %fusion.1 = (bf16[64,8192]{1,0:T(8,128)(2,1)}, bf16[64,8192]{1,0:T(8,128)(2,1)}, bf16[64,8192]{1,0:T(8,128)(2,1)}, bf16[64,8192]{1,0:T(8,128)(2,1)}) fusion(bf16[256,8192]{1,0:T(8,128)(2,1)} %bitcast.24), kind=kLoop, calls=%fused_computation.15 | loop fusion | bytes 8388608 | tf_op jit(solution)/shard_map/slice | solution.py:379
  59.5 1.4 collective-permute-start.1
  60.9 0.6 collective-permute-start.6
  61.5 1.4 collective-permute-start.5
  63.0 0.3 collective-permute-done.2
  63.3 0.5 collective-permute-start.4
  63.8 0.0 copy-done.5
  63.8 0.0 copy-done.4
  63.8 0.0 copy-done.2
  63.8 17.3 %weight_sums.1 = f32[192,128,128]{2,1,0:T(8,128)} custom-call(s32[192]{0:T(256)S(1)} %reshape_squeeze.6.rows, s32[192]{0:T(256)S(1)} %reshape_squeeze.7.cols, bf16[256,8192]{1,0:T(8,128)(2,1)S(1)} %bitcast.25, bf16[256,512]{1,0:T(8,128)(2,1)S(1)} %bitcast.28, f32[1,8192]{1,0:T(1,128)S(1)} %copy-done.5), custom_call_target="tpu_custom_call" | custom-call | flops 2147483648 | bytes 18874368 | tf_op jit(solution)/shard_map/weight_sums/pallas_call | solution.py:59
  81.1 0.0 copy-start.1
  81.1 4.6 %copy-done.1 = f32[192,128,128]{2,1,0:T(8,128)S(1)} copy-done((f32[192,128,128]{2,1,0:T(8,128)S(1)}, f32[192,128,128]{2,1,0:T(8,128)}, u32[]{:S(2)}) %copy-start.1) | copy-done | bytes 12582936
  85.7 0.0 copy-start.7
  85.7 83.6 %owner_sums.1 = f32[12,128,128]{2,1,0:T(8,128)S(1)} custom-call(f32[16,12,128,128]{3,2,1,0:T(8,128)S(1)} %bitcast.23), custom_call_target="tpu_custom_call" | custom-call | flops 10000000 | bytes 262144000 | tf_op jit(solution)/shard_map/owner_sums/pallas_call | solution.py:310
  169.3 0.0 copy-done.7
  169.3 0.3 multiply_reduce_fusion
  169.6 20.6 %all-gather.2 = f32[16,12,128]{2,1,0:T(8,128)S(1)} all-gather(f32[1,12,128]{2,1,0:T(8,128)S(1)} %bitcast.31), channel_id=1, replica_groups=mesh['section'=2,'fsdp'=16] {'fsdp'}, dimensions={0}, use_global_device_ids=true | all-gather | bytes 104448 | tf_op jit(solution)/shard_map/all_gather | solution.py:386
  190.2 0.2 select_reduce_fusion
  190.4 0.6 dynamic-slice_divide_fusion
  191.0 0.1 select_reduce_fusion.1.slot_of
  191.1 0.0 all-gather.5.cloned.1.call-done.tiles_ref
  191.1 0.0 copy-start.3
  191.1 2.8 %copy-done.3 = bf16[192,128,128]{2,1,0:T(8,128)(2,1)S(1)} copy-done((bf16[192,128,128]{2,1,0:T(8,128)(2,1)S(1)}, bf16[192,128,128]{2,1,0:T(8,128)(2,1)}, u32[]{:S(2)}) %copy-start.3) | copy-done | bytes 6291480
  193.9 6.1 %dense_weights.1.dense = bf16[8192,512]{1,0:T(8,128)(2,1)} custom-call(s32[256]{0:T(256)S(1)} %select_reduce_fusion.1.slot_of, bf16[192,128,128]{2,1,0:T(8,128)(2,1)S(1)} %copy-done.3), custom_call_target="tpu_custom_call" | custom-call | bytes 15728640 | tf_op jit(solution)/shard_map/dense_weights/pallas_call | solution.py:96
  200.0 0.0 collective-permute-done.3.gain_ref
  200.0 0.0 collective-permute-done.1.x_ref
  200.0 0.0 copy-start
  200.0 3.4 %copy-done = bf16[8192,512]{1,0:T(8,128)(2,1)S(1)} copy-done((bf16[8192,512]{1,0:T(8,128)(2,1)S(1)}, bf16[8192,512]{1,0:T(8,128)(2,1)}, u32[]{:S(2)}) %copy-start) | copy-done | bytes 8388632
  203.4 9.0 %input_part.4 = bf16[64,8192]{1,0:T(8,128)(2,1)S(1)} custom-call(bf16[64,8192]{1,0:T(8,128)(2,1)} %collective-permute-done.1.x_ref, bf16[64,512]{1,0:T(8,128)(2,1)S(1)} %get-tuple-element.13.grad_ref, f32[1,8192]{1,0:T(1,128)S(1)} %collective-permute-done.3.gain_ref, bf16[8192,512]{1,0:T(8,128)(2,1)S(1)} %copy-done), custom_call_target="tpu_custom_call" | custom-call | flops 536870912 | bytes 10485760 | tf_op jit(solution)/shard_map/input_part/pallas_call | solution.py:151
  212.4 0.0 collective-permute-done.6.x_ref
  212.4 9.0 %input_part.7 = bf16[64,8192]{1,0:T(8,128)(2,1)S(1)} custom-call(bf16[64,8192]{1,0:T(8,128)(2,1)} %collective-permute-done.6.x_ref, bf16[64,512]{1,0:T(8,128)(2,1)S(1)} %get-tuple-element.14.grad_ref, f32[1,8192]{1,0:T(1,128)S(1)} %collective-permute-done.3.gain_ref, bf16[8192,512]{1,0:T(8,128)(2,1)S(1)} %copy-done), custom_call_target="tpu_custom_call" | custom-call | flops 536870912 | bytes 10485760 | tf_op jit(solution)/shard_map/input_part/pallas_call | solution.py:151
  221.4 0.0 collective-permute-done.5.x_ref
  221.4 7.8 %input_part.6 = bf16[64,8192]{1,0:T(8,128)(2,1)S(1)} custom-call(bf16[64,8192]{1,0:T(8,128)(2,1)S(1)} %collective-permute-done.5.x_ref, bf16[64,512]{1,0:T(8,128)(2,1)S(1)} %get-tuple-element.15.grad_ref, f32[1,8192]{1,0:T(1,128)S(1)} %collective-permute-done.3.gain_ref, bf16[8192,512]{1,0:T(8,128)(2,1)S(1)} %copy-done), custom_call_target="tpu_custom_call" | custom-call | flops 536870912 | bytes 10485760 | tf_op jit(solution)/shard_map/input_part/pallas_call | solution.py:151
  229.2 0.0 collective-permute-done.4.x_ref
  229.3 7.8 %input_part.5 = bf16[64,8192]{1,0:T(8,128)(2,1)S(1)} custom-call(bf16[64,8192]{1,0:T(8,128)(2,1)S(1)} %collective-permute-done.4.x_ref, bf16[64,512]{1,0:T(8,128)(2,1)S(1)} %get-tuple-element.16.grad_ref, f32[1,8192]{1,0:T(1,128)S(1)} %collective-permute-done.3.gain_ref, bf16[8192,512]{1,0:T(8,128)(2,1)S(1)} %copy-done), custom_call_target="tpu_custom_call" | custom-call | flops 536870912 | bytes 10485760 | tf_op jit(solution)/shard_map/input_part/pallas_call | solution.py:151
  237.1 2.3 maximum_bitcast_fusion
  239.3 0.9 copy.18
  (7 shorter events, 0.1 us)
Async XLA Ops:
  7.2 56.6 %copy-start.5 = (f32[1,8192]{1,0:T(1,128)S(1)}, f32[1,8192]{1,0:T(1,128)}, u32[]{:S(2)}) copy-start(f32[1,8192]{1,0:T(1,128)} %gain_ref.1) | copy-start | bytes 98308
  7.2 56.6 %copy-start.4 = (bf16[1,256,512]{2,1,0:T(8,128)(2,1)S(1)}, bf16[1,256,512]{2,1,0:T(8,128)(2,1)}, u32[]{:S(2)}) copy-start(bf16[1,256,512]{2,1,0:T(8,128)(2,1)} %param.7) | copy-start | bytes 786436
  7.2 183.9 %all-gather.5.cloned.1.call-start = ((), (), s32[]{:S(2)}) async-start(), calls=%async_computation | async-start | bytes 6684672 | tf_op jit(solution)/shard_map/all_gather | solution.py:366
  7.2 44.6 %collective-permute-start = (bf16[12,128,128]{2,1,0:T(8,128)(2,1)}, bf16[12,128,128]{2,1,0:T(8,128)(2,1)S(1)}, u32[]{:S(2)}, u32[]{:S(2)}) collective-permute-start(bf16[12,128,128]{2,1,0:T(8,128)(2,1)} %bitcast.29), channel_id=1, source_target_pairs={{0,16},{16,0},{1,17},{17,1},{2,18},{18,2},{3,19},{19,3},{4,20},{20... | collective-permute-start | bytes 1179656 | tf_op jit(solution)/shard_map/ppermute | solution.py:353
  51.9 0.7 copy-start.6
  52.7 147.3 %collective-permute-start.3 = (f32[1,8192]{1,0:T(1,128)}, f32[1,8192]{1,0:T(1,128)S(1)}, u32[]{:S(2)}, u32[]{:S(2)}) collective-permute-start(f32[1,8192]{1,0:T(1,128)} %gain_ref.1), channel_id=1, source_target_pairs={{0,16},{16,0},{1,17},{17,1},{2,18},{18,2},{3,19},{19,3},{4,20},{20... | collective-permute-start | bytes 98312 | tf_op jit(solution)/shard_map/ppermute | solution.py:353
  54.2 9.1 %collective-permute-start.2 = (bf16[256,512]{1,0:T(8,128)(2,1)}, bf16[256,512]{1,0:T(8,128)(2,1)S(1)}, u32[]{:S(2)}, u32[]{:S(2)}) collective-permute-start(bf16[256,512]{1,0:T(8,128)(2,1)} %bitcast.27), channel_id=1, source_target_pairs={{0,16},{16,0},{1,17},{17,1},{2,18},{18,2},{3,19},{19,3},{4,20},{20... | collective-permute-start | bytes 786440 | tf_op jit(solution)/shard_map/ppermute | solution.py:353
  54.9 8.9 %copy-start.2 = (bf16[1,256,8192]{2,1,0:T(8,128)(2,1)S(1)}, bf16[1,256,8192]{2,1,0:T(8,128)(2,1)}, u32[]{:S(2)}) copy-start(bf16[1,256,8192]{2,1,0:T(8,128)(2,1)} %param.6) | copy-start | bytes 12582916
  59.5 140.5 %collective-permute-start.1 = (bf16[64,8192]{1,0:T(8,128)(2,1)}, bf16[64,8192]{1,0:T(8,128)(2,1)}, u32[]{:S(2)}, u32[]{:S(2)}) collective-permute-start(bf16[64,8192]{1,0:T(8,128)(2,1)} %get-tuple-element.9), channel_id=1, source_target_pairs={{0,16},{16,0},{1,17},{17,1},{2,18},{18,2},{3,19},{19,3},{4,20},{20... | collective-permute-start | bytes 3145736 | tf_op jit(solution)/shard_map/ppermute | solution.py:353
  60.9 151.5 %collective-permute-start.6 = (bf16[64,8192]{1,0:T(8,128)(2,1)}, bf16[64,8192]{1,0:T(8,128)(2,1)}, u32[]{:S(2)}, u32[]{:S(2)}) collective-permute-start(bf16[64,8192]{1,0:T(8,128)(2,1)} %get-tuple-element.10), channel_id=1, source_target_pairs={{0,16},{16,0},{1,17},{17,1},{2,18},{18,2},{3,19},{19,3},{4,20},{20... | collective-permute-start | bytes 3145736 | tf_op jit(solution)/shard_map/ppermute | solution.py:353
  61.5 159.9 %collective-permute-start.5 = (bf16[64,8192]{1,0:T(8,128)(2,1)}, bf16[64,8192]{1,0:T(8,128)(2,1)S(1)}, u32[]{:S(2)}, u32[]{:S(2)}) collective-permute-start(bf16[64,8192]{1,0:T(8,128)(2,1)} %get-tuple-element.11), channel_id=1, source_target_pairs={{0,16},{16,0},{1,17},{17,1},{2,18},{18,2},{3,19},{19,3},{4,20},{20... | collective-permute-start | bytes 3145736 | tf_op jit(solution)/shard_map/ppermute | solution.py:353
  63.3 166.0 %collective-permute-start.4 = (bf16[64,8192]{1,0:T(8,128)(2,1)}, bf16[64,8192]{1,0:T(8,128)(2,1)S(1)}, u32[]{:S(2)}, u32[]{:S(2)}) collective-permute-start(bf16[64,8192]{1,0:T(8,128)(2,1)} %get-tuple-element.12), channel_id=1, source_target_pairs={{0,16},{16,0},{1,17},{17,1},{2,18},{18,2},{3,19},{19,3},{4,20},{20... | collective-permute-start | bytes 3145736 | tf_op jit(solution)/shard_map/ppermute | solution.py:353
  81.1 4.6 %copy-start.1 = (f32[192,128,128]{2,1,0:T(8,128)S(1)}, f32[192,128,128]{2,1,0:T(8,128)}, u32[]{:S(2)}) copy-start(f32[192,128,128]{2,1,0:T(8,128)} %weight_sums.1) | copy-start | bytes 37748740
  85.7 83.6 %copy-start.7 = (bf16[1,12,128,128]{3,2,1,0:T(8,128)(2,1)S(1)}, bf16[1,12,128,128]{3,2,1,0:T(8,128)(2,1)}, u32[]{:S(2)}) copy-start(bf16[1,12,128,128]{3,2,1,0:T(8,128)(2,1)} %param.9) | copy-start | bytes 1179652
  191.1 2.8 %copy-start.3 = (bf16[192,128,128]{2,1,0:T(8,128)(2,1)S(1)}, bf16[192,128,128]{2,1,0:T(8,128)(2,1)}, u32[]{:S(2)}) copy-start(bf16[192,128,128]{2,1,0:T(8,128)(2,1)} %all-gather.5.cloned.1.call-done.tiles_ref) | copy-start | bytes 18874372
  200.0 3.4 %copy-start = (bf16[8192,512]{1,0:T(8,128)(2,1)S(1)}, bf16[8192,512]{1,0:T(8,128)(2,1)}, u32[]{:S(2)}) copy-start(bf16[8192,512]{1,0:T(8,128)(2,1)} %dense_weights.1.dense) | copy-start | bytes 25165828
Sparse Core Ops, SparseCore 0:
  52.8 69.6 all-gather.4

commit v3 on v2

--- a/solution.py
+++ b/solution.py
@@ -74,42 +74,25 @@
     )(rows, cols, x, grads, gain)
 
 
-def dense_kernel(slot_of, tiles_ref, out_ref):
+def input_kernel(slot_of, x_ref, grad_ref, gain_ref, tiles_ref, out_ref, dense, feature):
     side = tiles_ref.shape[1]
-    first = pl.program_id(0) * (out_ref.shape[0] // side)
-    col_blocks = out_ref.shape[1] // side
-
-    def build(row, carry):
-        at_row = pl.ds(pl.multiple_of(row * side, side), side)
-        for col in range(col_blocks):
-            slot = slot_of[(first + row) * col_blocks + col]
-            block = tiles_ref[jnp.maximum(slot, 0)]
-            out_ref[at_row, col * side : (col + 1) * side] = jnp.where(
-                slot >= 0, block, jnp.zeros_like(block)
-            )
-        return carry
-
-    lax.fori_loop(0, out_ref.shape[0] // side, build, 0)
-
-
-def dense_weights(tiles, slot_of, width, keys):
-    return pl.pallas_call(
-        dense_kernel,
-        out_shape=jax.ShapeDtypeStruct((width, keys), tiles.dtype),
-        grid_spec=pltpu.PrefetchScalarGridSpec(
-            num_scalar_prefetch=1,
-            grid=(8,),
-            in_specs=[pl.BlockSpec(tiles.shape, lambda i, s: (0, 0, 0))],
-            out_specs=pl.BlockSpec((width // 8, keys), lambda i, s: (i, 0)),
-        ),
-        compiler_params=pltpu.CompilerParams(vmem_limit_bytes=40 * 2**20),
-        cost_estimate=pl.CostEstimate(flops=0, bytes_accessed=15 * 2**20, transcendentals=0),
-        name="dense_weights",
-    )(slot_of, tiles)
-
-
-def input_kernel(x_ref, grad_ref, gain_ref, dense, out_ref, feature):
     tokens, width = x_ref.shape
+    keys = grad_ref.shape[1]
+    col_blocks = keys // side
+
+    @pl.when(pl.program_id(0) == 0)
+    def _():
+        def build(row, carry):
+            at_row = pl.ds(pl.multiple_of(row * side, side), side)
+            for col in range(col_blocks):
+                slot = slot_of[row * col_blocks + col]
+                block = tiles_ref[jnp.maximum(slot, 0)]
+                dense[at_row, col * side : (col + 1) * side] = jnp.where(
+                    slot >= 0, block, jnp.zeros_like(block)
+                )
+            return carry
+
+        lax.fori_loop(0, width // side, build, 0)
 
     def squares(step, total):
         wide = x_ref[:, pl.ds(pl.multiple_of(step * WIDE, WIDE), WIDE)].astype(jnp.float32)
@@ -144,28 +127,84 @@
     lax.fori_loop(0, width // WIDE, finish, 0)
 
 
-def input_part(x, grads, gain, dense):
+def input_part(x, grads, gain, tiles, slot_of):
     tokens, width = x.shape
     keys = grads.shape[1]
-    block = min(tokens, 64)
+    block = min(tokens, 128)
     return pl.pallas_call(
         input_kernel,
         out_shape=jax.ShapeDtypeStruct((tokens, width), jnp.bfloat16),
-        grid=(tokens // block,),
-        in_specs=[
-            pl.BlockSpec((block, width), lambda i: (i, 0)),
-            pl.BlockSpec((block, keys), lambda i: (i, 0)),
-            pl.BlockSpec((1, width), lambda i: (0, 0)),
-            pl.BlockSpec(dense.shape, lambda i: (0, 0)),
-        ],
-        out_specs=pl.BlockSpec((block, width), lambda i: (i, 0)),
-        scratch_shapes=[pltpu.VMEM((block, width), jnp.float32)],
+        grid_spec=pltpu.PrefetchScalarGridSpec(
+            num_scalar_prefetch=1,
+            grid=(tokens // block,),
+            in_specs=[
+                pl.BlockSpec((block, width), lambda i, s: (i, 0)),
+                pl.BlockSpec((block, keys), lambda i, s: (i, 0)),
+                pl.BlockSpec((1, width), lambda i, s: (0, 0)),
+                pl.BlockSpec(tiles.shape, lambda i, s: (0, 0, 0)),
+            ],
+            out_specs=pl.BlockSpec((block, width), lambda i, s: (i, 0)),
+            scratch_shapes=[
+                pltpu.VMEM((width, keys), jnp.bfloat16),
+                pltpu.VMEM((block, width), jnp.float32),
+            ],
+        ),
         compiler_params=pltpu.CompilerParams(vmem_limit_bytes=40 * 2**20),
         cost_estimate=pl.CostEstimate(
             flops=2 * tokens * width * keys, bytes_accessed=10 * 2**20, transcendentals=0
         ),
         name="input_part",
-    )(x, grads, gain, dense)
+    )(slot_of, x, grads, gain, tiles)
+
+
+def share_kernel(owners, value_ref, out_ref, held, send, recv):
+    index = lax.axis_index("fsdp")
+
+    def copy(ahead):
+        return pltpu.make_async_remote_copy(
+            src_ref=value_ref,
+            dst_ref=held.at[index],
+            send_sem=send.at[ahead - 1],
+            recv_sem=recv.at[ahead - 1],
+            device_id={"fsdp": (index + ahead) % owners},
+            device_id_type=pl.DeviceIdType.MESH,
+        )
+
+    barrier = pltpu.get_barrier_semaphore()
+    for ahead in range(1, owners):
+        pl.semaphore_signal(
+            barrier,
+            inc=1,
+            device_id={"fsdp": (index + ahead) % owners},
+            device_id_type=pl.DeviceIdType.MESH,
+        )
+    pl.semaphore_wait(barrier, owners - 1)
+    for ahead in range(1, owners):
+        copy(ahead).start()
+    held[index] = value_ref[...]
+    for ahead in range(1, owners):
+        copy(ahead).wait_recv()
+    out_ref[...] = held[...]
+    for ahead in range(1, owners):
+        copy(ahead).wait_send()
+
+
+def spread(value, collective_id):
+    owners = lax.axis_size("fsdp")
+    return pl.pallas_call(
+        functools.partial(share_kernel, owners),
+        out_shape=jax.ShapeDtypeStruct((owners,) + value.shape, value.dtype),
+        in_specs=[pl.BlockSpec(memory_space=pltpu.VMEM)],
+        out_specs=pl.BlockSpec(memory_space=pltpu.VMEM),
+        scratch_shapes=[
+            pltpu.VMEM((owners,) + value.shape, value.dtype),
+            pltpu.SemaphoreType.DMA((owners - 1,)),
+            pltpu.SemaphoreType.DMA((owners - 1,)),
+        ],
+        compiler_params=pltpu.CompilerParams(collective_id=collective_id, has_side_effects=True),
+        cost_estimate=pl.CostEstimate(flops=0, bytes_accessed=10 * 2**20, transcendentals=0),
+        name="share_places" if collective_id == 1 else "share_sums",
+    )(value)
 
 
 def owner_kernel(lines, levels, sums, out_ref, half, near, stage, across, up, down, load, sems):
@@ -353,16 +392,15 @@
     shift = lambda value: lax.ppermute(value, "section", behind)
 
     next_tiles = shift(own_tiles)
-    places = lax.all_gather(
-        jnp.concatenate([tile_rows, tile_cols]), ("section", "fsdp"), axis=0, tiled=False
-    ).reshape(sections, owners, 2, -1)
-    next_places = lax.dynamic_index_in_dim(places, (section + 1) % sections, 0, keepdims=False)
-    places = lax.dynamic_index_in_dim(places, section, 0, keepdims=False)
+    slots = tile_rows.shape[1]
+    listed = jnp.concatenate([tile_rows, tile_cols])
+    places = spread(jnp.pad(listed, ((0, 6), (0, 128 - slots))), 1)[:, :2, :slots]
+    next_places = shift(places)
     rows, cols = places[:, 0].reshape(-1), places[:, 1].reshape(-1)
     next_ids = jnp.where(
         next_places[:, 0] >= 0, next_places[:, 0] * col_blocks + next_places[:, 1], -1
     ).reshape(-1)
-    next_tiles, next_ids = lax.optimization_barrier((next_tiles, next_ids))
+    next_tiles, places = lax.optimization_barrier((next_tiles, places))
     all_tiles = lax.all_gather(next_tiles, "fsdp", axis=0, tiled=True)
     hit = next_ids[None, :] == jnp.arange(row_blocks * col_blocks, dtype=jnp.int32)[:, None]
     slot_of = jnp.max(
@@ -371,19 +409,15 @@
 
     next_gain = shift(gain)
     next_grads = shift(grads)
-    parts = 4 if tokens % 256 == 0 else 1
-    step = tokens // parts
-    arrived = []
     x_later, _ = lax.optimization_barrier((x, next_tiles))
-    for part in range(parts):
-        arrived.append(shift(x_later[part * step : (part + 1) * step]))
+    arrived = shift(x_later)
 
     x_first, _ = lax.optimization_barrier((x, next_tiles))
     sums = weight_sums(x_first, grads, gain, rows, cols, owners, side)
     weight_grad = reduce_to_owners(sums)
 
     along = jnp.sum(weight_grad * own_tiles.astype(jnp.float32), axis=-1)
-    along = lax.all_gather(along, "fsdp", axis=0, tiled=True)
+    along = spread(jnp.pad(along, ((0, -slots % 8), (0, 0))), 2)[:, :slots].reshape(-1, side)
     share = row_blocks // owners
     mine = index * share + jnp.arange(share, dtype=jnp.int32)
     gain_share = jnp.sum(
@@ -391,13 +425,7 @@
     ).reshape(-1)
     gain_share = gain_share / lax.dynamic_slice_in_dim(gain[0], index * share * side, share * side)
 
-    dense = dense_weights(all_tiles, slot_of, width, grads.shape[1])
-    upstream = jnp.concatenate(
-        [
-            input_part(got, next_grads[part * step : (part + 1) * step], next_gain, dense)
-            for part, got in enumerate(arrived)
-        ]
-    )
+    upstream = input_part(arrived, next_grads, next_gain, all_tiles, slot_of)
     return (weight_grad[None], gain_share[None], upstream[None])
 
 

time: 247 us -> 259 us (1.049)
  waiting for transfers between devices: 0.36 us -> 88.7 us
  blocking collectives: 61.4 us -> 0 us
  Pallas kernels: 141 us -> 129 us
    ppermute x7 -> x5, waiting for transfers between devices: 0.33 us -> 88.7 us  [on_device(): shift = lambda value: lax.ppermute(value, 'section', behind)]
    all_gather x2 -> x0, blocking collectives: 61.4 us -> none  [the longest x1 40.8 us: on_device(): lax.all_gather(jnp.concatenate([tile_rows, tile_cols]), ('section', 'fsdp...]
    pallas_call x1, Pallas kernels: 83.6 us -> 70.8 us  [reduce_to_owners(): pl.pallas_call(functools.partial(owner_kernel, lines, levels), out_shape=...]
    pallas_call x1 -> x2, Pallas kernels: 6.1 us -> 17.5 us  [spread(): pl.pallas_call(functools.partial(share_kernel, owners), out_shape=jax.Sha...]
    pallas_call x4 -> x1, Pallas kernels: 33.6 us -> 23.5 us  [input_part(): pl.pallas_call(input_kernel, out_shape=jax.ShapeDtypeStruct((tokens, widt...]
    slice x2 -> x1, local copies, waits for them, and re-layouts: 4.5 us -> 0.85 us  [on_device(): spread(jnp.pad(listed, ((0, 6), (0, 128 - slots))), 1)[:, :2, :slots]]
    ppermute x7 -> x5, starting transfers between devices: 9.02 us -> 7.13 us  [on_device(): shift = lambda value: lax.ppermute(value, 'section', behind)]
    unnamed x18 -> x15, local copies, waits for them, and re-layouts: 12.4 us -> 12.9 us
  transfers between devices with their start and end apart: 8 -> 6, of which waited for: 1 -> 1; matrix products, arithmetic and copies ran while one was open for 3% -> 3% of each run, Pallas kernels for 54% -> 41%
where the time goes in v3:
time: 259 us
  Pallas kernels  129 us (50%)
  waiting for transfers between devices  88.7 us (34%)
  local copies, waits for them, and re-layouts  17 us (7%)
  between operations  14.1 us (5%)
  starting transfers between devices  7.17 us (3%)
  other arithmetic  2.65 us (1%)
    ppermute x5, waiting for transfers between devices, on_device(): shift = lambda value: lax.ppermute(value, 'section', behind)  88.7 us
    pallas_call x1, Pallas kernels, reduce_to_owners(): pl.pallas_call(functools.partial(owner_kernel, lines, levels), out_shape=...  70.8 us
    pallas_call x1, Pallas kernels, input_part(): pl.pallas_call(input_kernel, out_shape=jax.ShapeDtypeStruct((tokens, widt...  23.5 us
    pallas_call x2, Pallas kernels, spread(): pl.pallas_call(functools.partial(share_kernel, owners), out_shape=jax.Sha...  17.5 us
    pallas_call x1, Pallas kernels, weight_sums(): pl.pallas_call(weight_kernel, out_shape=jax.ShapeDtypeStruct((owners * sl...  17.3 us
    unnamed x15, local copies, waits for them, and re-layouts  12.9 us
    ppermute x5, starting transfers between devices, on_device(): shift = lambda value: lax.ppermute(value, 'section', behind)  7.13 us
  transfers between devices with their start and end apart: 6, of which 1 were waited for; matrix products, arithmetic and copies ran while one was open for 3% of the time, Pallas kernels for 41%

profile of v3, /device:TPU:0, one launch (start us, length us, event | category | flops | bytes accessed | tf_op | source)
XLA Modules:
  0.0 258.9 jit_solution(9830006295208623498)
XLA Ops:
  7.2 0.0 all-gather.2.cloned.1.call-start
  7.2 3.0 %collective-permute-start = (bf16[12,128,128]{2,1,0:T(8,128)(2,1)}, bf16[12,128,128]{2,1,0:T(8,128)(2,1)S(1)}, u32[]{:S(2)}, u32[]{:S(2)}) collective-permute-start(bf16[12,128,128]{2,1,0:T(8,128)(2,1)} %bitcast.17), channel_id=1, source_target_pairs={{0,16},{16,0},{1,17},{17,1},{2,18},{18,2},{3,19},{19,3},{4,20},{20... | collective-permute-start | bytes 1179656 | tf_op jit(solution)/shard_map/ppermute | solution.py:392
  10.2 0.7 pad_add_fusion
  10.9 0.6 pad.8.value_ref
  11.5 8.7 %share_places.1 = s32[16,8,128]{2,1,0:T(8,128)} custom-call(s32[8,128]{1,0:T(8,128)} %pad.8.value_ref), custom_call_target="tpu_custom_call" | custom-call | bytes 10485760 | tf_op jit(solution)/shard_map/share_places/pallas_call | solution.py:194
  20.2 0.8 slice.23
  21.1 0.0 collective-permute-done
  21.1 0.0 copy-start.5
  21.1 0.7 copy-done.5
  21.8 0.0 all-gather.2.cloned.1.call-update
  21.8 0.6 collective-permute-start.2
  22.4 1.5 collective-permute-start.1
  23.9 0.5 collective-permute-start.3
  24.5 1.5 collective-permute-start.4
  26.0 1.0 slice_reduce_fusion
  26.9 0.1 reshape_squeeze.6.rows
  27.0 0.1 broadcast_compare_fusion
  27.1 0.1 reshape_squeeze.7.cols
  27.2 88.7 %collective-permute-done.1 = s32[16,2,12]{2,1,0:T(2,128)S(1)} collective-permute-done((s32[16,2,12]{2,1,0:T(2,128)S(1)}, s32[16,2,12]{2,1,0:T(2,128)S(1)}, u32[]{:S(2)}, u32[]{:S(2)}) %collective-permute-start.1) | collective-permute-done | bytes 1568 | tf_op jit(solution)/shard_map/ppermute | solution.py:392
  115.9 0.1 select_n.25
  116.0 0.1 select_reduce_fusion.1.slot_of
  116.1 0.0 copy-start.2
  116.2 2.2 copy-done.2
  118.3 0.0 copy-start.3
  118.3 0.9 copy-done.3
  119.3 0.0 copy-start.4
  119.3 0.8 copy-done.4
  120.0 17.3 %weight_sums.1 = f32[192,128,128]{2,1,0:T(8,128)} custom-call(s32[192]{0:T(256)S(1)} %reshape_squeeze.6.rows, s32[192]{0:T(256)S(1)} %reshape_squeeze.7.cols, bf16[256,8192]{1,0:T(8,128)(2,1)S(1)} %bitcast.12, bf16[256,512]{1,0:T(8,128)(2,1)S(1)} %bitcast.14, f32[1,8192]{1,0:T(1,128)S(1)} %copy-done.4), custom_call_target="tpu_custom_call" | custom-call | flops 2147483648 | bytes 18874368 | tf_op jit(solution)/shard_map/weight_sums/pallas_call | solution.py:59
  137.3 0.0 copy-start
  137.3 4.6 %copy-done = f32[192,128,128]{2,1,0:T(8,128)S(1)} copy-done((f32[192,128,128]{2,1,0:T(8,128)S(1)}, f32[192,128,128]{2,1,0:T(8,128)}, u32[]{:S(2)}) %copy-start) | copy-done | bytes 12582936
  141.9 0.0 copy-start.6
  141.9 70.8 %owner_sums.1 = f32[12,128,128]{2,1,0:T(8,128)S(1)} custom-call(f32[16,12,128,128]{3,2,1,0:T(8,128)S(1)} %bitcast.9), custom_call_target="tpu_custom_call" | custom-call | flops 10000000 | bytes 262144000 | tf_op jit(solution)/shard_map/owner_sums/pallas_call | solution.py:349
  212.7 0.0 copy-done.6
  212.7 0.3 multiply_reduce_fusion
  213.0 0.6 pad.9.value_ref
  213.7 8.8 %share_sums.1 = f32[16,16,128]{2,1,0:T(8,128)} custom-call(f32[16,128]{1,0:T(8,128)} %pad.9.value_ref), custom_call_target="tpu_custom_call" | custom-call | bytes 10485760 | tf_op jit(solution)/shard_map/share_sums/pallas_call | solution.py:194
  222.5 0.9 broadcast_in_dim.51
  223.4 0.2 select_reduce_fusion
  223.6 1.3 dynamic-slice_divide_fusion
  224.9 0.0 collective-permute-done.4.gain_ref
  224.9 0.0 collective-permute-done.3.grad_ref
  224.9 0.0 collective-permute-done.2.x_ref
  224.9 0.0 all-gather.2.cloned.1.call-done.tiles_ref
  224.9 0.0 copy-start.1
  224.9 2.8 %copy-done.1 = bf16[192,128,128]{2,1,0:T(8,128)(2,1)S(1)} copy-done((bf16[192,128,128]{2,1,0:T(8,128)(2,1)S(1)}, bf16[192,128,128]{2,1,0:T(8,128)(2,1)}, u32[]{:S(2)}) %copy-start.1) | copy-done | bytes 6291480
  227.7 23.5 %input_part.1 = bf16[256,8192]{1,0:T(8,128)(2,1)} custom-call(s32[256]{0:T(256)S(1)} %select_reduce_fusion.1.slot_of, bf16[256,8192]{1,0:T(8,128)(2,1)} %collective-permute-done.2.x_ref, bf16[256,512]{1,0:T(8,128)(2,1)S(1)} %collective-permute-done.3.grad_ref, f32[1,8192]{1,0:T(1,128)S(1)} %collective-permute-done.4.gain_ref, ...), custom_call_target="tpu_custom_call" | custom-call | flops 2147483648 | bytes 10485760 | tf_op jit(solution)/shard_map/input_part/pallas_call | solution.py:134
  251.2 0.9 copy.10
  (2 shorter events, 0.0 us)
Async XLA Ops:
  7.2 217.7 %all-gather.2.cloned.1.call-start = ((), (), s32[]{:S(2)}) async-start(), calls=%async_computation | async-start | bytes 6684672 | tf_op jit(solution)/shard_map/all_gather | solution.py:404
  7.2 13.9 %collective-permute-start = (bf16[12,128,128]{2,1,0:T(8,128)(2,1)}, bf16[12,128,128]{2,1,0:T(8,128)(2,1)S(1)}, u32[]{:S(2)}, u32[]{:S(2)}) collective-permute-start(bf16[12,128,128]{2,1,0:T(8,128)(2,1)} %bitcast.17), channel_id=1, source_target_pairs={{0,16},{16,0},{1,17},{17,1},{2,18},{18,2},{3,19},{19,3},{4,20},{20... | collective-permute-start | bytes 1179656 | tf_op jit(solution)/shard_map/ppermute | solution.py:392
  21.1 0.7 copy-start.5
  21.8 203.0 %collective-permute-start.2 = (bf16[256,8192]{1,0:T(8,128)(2,1)}, bf16[256,8192]{1,0:T(8,128)(2,1)}, u32[]{:S(2)}, u32[]{:S(2)}) collective-permute-start(bf16[256,8192]{1,0:T(8,128)(2,1)} %bitcast.11), channel_id=1, source_target_pairs={{0,16},{16,0},{1,17},{17,1},{2,18},{18,2},{3,19},{19,3},{4,20},{20... | collective-permute-start | bytes 12582920 | tf_op jit(solution)/shard_map/ppermute | solution.py:392
  22.4 93.5 %collective-permute-start.1 = (s32[16,2,12]{2,1,0:T(2,128)S(1)}, s32[16,2,12]{2,1,0:T(2,128)S(1)}, u32[]{:S(2)}, u32[]{:S(2)}) collective-permute-start(s32[16,2,12]{2,1,0:T(2,128)S(1)} %slice.23), channel_id=1, source_target_pairs={{0,16},{16,0},{1,17},{17,1},{2,18},{18,2},{3,19},{19,3},{4,20},{20... | collective-permute-start | bytes 4616 | tf_op jit(solution)/shard_map/ppermute | solution.py:392
  23.9 200.9 %collective-permute-start.3 = (bf16[256,512]{1,0:T(8,128)(2,1)}, bf16[256,512]{1,0:T(8,128)(2,1)S(1)}, u32[]{:S(2)}, u32[]{:S(2)}) collective-permute-start(bf16[256,512]{1,0:T(8,128)(2,1)} %bitcast.13), channel_id=1, source_target_pairs={{0,16},{16,0},{1,17},{17,1},{2,18},{18,2},{3,19},{19,3},{4,20},{20... | collective-permute-start | bytes 786440 | tf_op jit(solution)/shard_map/ppermute | solution.py:392
  24.5 200.4 %collective-permute-start.4 = (f32[1,8192]{1,0:T(1,128)}, f32[1,8192]{1,0:T(1,128)S(1)}, u32[]{:S(2)}, u32[]{:S(2)}) collective-permute-start(f32[1,8192]{1,0:T(1,128)} %gain_ref.1), channel_id=1, source_target_pairs={{0,16},{16,0},{1,17},{17,1},{2,18},{18,2},{3,19},{19,3},{4,20},{20... | collective-permute-start | bytes 98312 | tf_op jit(solution)/shard_map/ppermute | solution.py:392
  116.1 2.2 copy-start.2
  118.3 0.9 copy-start.3
  119.3 0.8 copy-start.4
  137.3 4.6 %copy-start = (f32[192,128,128]{2,1,0:T(8,128)S(1)}, f32[192,128,128]{2,1,0:T(8,128)}, u32[]{:S(2)}) copy-start(f32[192,128,128]{2,1,0:T(8,128)} %weight_sums.1) | copy-start | bytes 37748740
  141.9 70.8 %copy-start.6 = (bf16[1,12,128,128]{3,2,1,0:T(8,128)(2,1)S(1)}, bf16[1,12,128,128]{3,2,1,0:T(8,128)(2,1)}, u32[]{:S(2)}) copy-start(bf16[1,12,128,128]{3,2,1,0:T(8,128)(2,1)} %param.9) | copy-start | bytes 1179652
  224.9 2.8 %copy-start.1 = (bf16[192,128,128]{2,1,0:T(8,128)(2,1)S(1)}, bf16[192,128,128]{2,1,0:T(8,128)(2,1)}, u32[]{:S(2)}) copy-start(bf16[192,128,128]{2,1,0:T(8,128)(2,1)} %all-gather.2.cloned.1.call-done.tiles_ref) | copy-start | bytes 18874372
Sparse Core Ops, SparseCore 0:
  22.0 61.8 all-gather.1

commit v4 on v3

--- a/solution.py
+++ b/solution.py
@@ -402,17 +402,17 @@
     ).reshape(-1)
     next_tiles, places = lax.optimization_barrier((next_tiles, places))
     all_tiles = lax.all_gather(next_tiles, "fsdp", axis=0, tiled=True)
+    next_gain = shift(gain)
+    next_grads = shift(grads)
+    x_later, _, next_ids = lax.optimization_barrier((x, next_tiles, next_ids))
+    arrived = shift(x_later)
+
     hit = next_ids[None, :] == jnp.arange(row_blocks * col_blocks, dtype=jnp.int32)[:, None]
     slot_of = jnp.max(
         jnp.where(hit, jnp.arange(next_ids.shape[0], dtype=jnp.int32)[None, :], -1), axis=1
     )
 
-    next_gain = shift(gain)
-    next_grads = shift(grads)
-    x_later, _ = lax.optimization_barrier((x, next_tiles))
-    arrived = shift(x_later)
-
-    x_first, _ = lax.optimization_barrier((x, next_tiles))
+    x_first, _, _ = lax.optimization_barrier((x, next_tiles, next_ids))
     sums = weight_sums(x_first, grads, gain, rows, cols, owners, side)
     weight_grad = reduce_to_owners(sums)
 

time: 259 us -> 191 us (0.74)
  waiting for transfers between devices: 88.7 us -> 3.25 us
  Pallas kernels: 129 us -> 146 us
    ppermute x5, waiting for transfers between devices: 88.7 us -> 3.21 us  [on_device(): shift = lambda value: lax.ppermute(value, 'section', behind)]
    pallas_call x1, Pallas kernels: 70.8 us -> 88.4 us  [reduce_to_owners(): pl.pallas_call(functools.partial(owner_kernel, lines, levels), out_shape=...]
  transfers between devices with their start and end apart: 6 -> 6, of which waited for: 1 -> 1; matrix products, arithmetic and copies ran while one was open for 3% -> 4% of each run, Pallas kernels for 41% -> 64%
where the time goes in v4:
time: 191 us; the launch traced here: 190 us
  Pallas kernels  146 us (76%)
  local copies, waits for them, and re-layouts  17.7 us (9%)
  between operations  14.2 us (7%)
  starting transfers between devices  6.26 us (3%)
  waiting for transfers between devices  3.25 us (2%)
  other arithmetic  2.63 us (1%)
    pallas_call x1, Pallas kernels, reduce_to_owners(): pl.pallas_call(functools.partial(owner_kernel, lines, levels), out_shape=...  88.4 us
    pallas_call x1, Pallas kernels, input_part(): pl.pallas_call(input_kernel, out_shape=jax.ShapeDtypeStruct((tokens, widt...  23.5 us
    pallas_call x1, Pallas kernels, weight_sums(): pl.pallas_call(weight_kernel, out_shape=jax.ShapeDtypeStruct((owners * sl...  17.3 us
    pallas_call x2, Pallas kernels, spread(): pl.pallas_call(functools.partial(share_kernel, owners), out_shape=jax.Sha...  16.8 us
    unnamed x15, local copies, waits for them, and re-layouts  13.5 us
    ppermute x5, starting transfers between devices, on_device(): shift = lambda value: lax.ppermute(value, 'section', behind)  6.23 us
  transfers between devices with their start and end apart: 6, of which 1 were waited for; matrix products, arithmetic and copies ran while one was open for 4% of the time, Pallas kernels for 64%

profile of v4, /device:TPU:0, one launch (start us, length us, event | category | flops | bytes accessed | tf_op | source)
XLA Modules:
  0.0 190.0 jit_solution(18387150769562771121)
XLA Ops:
  7.2 0.0 all-gather.2.cloned.1.call-start
  7.2 3.0 %collective-permute-start = (bf16[12,128,128]{2,1,0:T(8,128)(2,1)}, bf16[12,128,128]{2,1,0:T(8,128)(2,1)S(1)}, u32[]{:S(2)}, u32[]{:S(2)}) collective-permute-start(bf16[12,128,128]{2,1,0:T(8,128)(2,1)} %bitcast.17), channel_id=1, source_target_pairs={{0,16},{16,0},{1,17},{17,1},{2,18},{18,2},{3,19},{19,3},{4,20},{20... | collective-permute-start | bytes 1179656 | tf_op jit(solution)/shard_map/ppermute | solution.py:392
  10.2 0.7 pad_add_fusion
  10.9 0.6 pad.8.value_ref
  11.5 8.7 %share_places.1 = s32[16,8,128]{2,1,0:T(8,128)} custom-call(s32[8,128]{1,0:T(8,128)} %pad.8.value_ref), custom_call_target="tpu_custom_call" | custom-call | bytes 10485760 | tf_op jit(solution)/shard_map/share_places/pallas_call | solution.py:194
  20.2 0.8 slice.23
  21.1 0.0 collective-permute-done
  21.1 0.0 copy-start.5
  21.1 0.7 copy-done.5
  21.8 0.0 all-gather.2.cloned.1.call-update
  21.8 0.6 collective-permute-start.1
  22.4 3.2 %collective-permute-done.1 = s32[16,2,12]{2,1,0:T(2,128)S(1)} collective-permute-done((s32[16,2,12]{2,1,0:T(2,128)S(1)}, s32[16,2,12]{2,1,0:T(2,128)S(1)}, u32[]{:S(2)}, u32[]{:S(2)}) %collective-permute-start.1) | collective-permute-done | bytes 1568 | tf_op jit(solution)/shard_map/ppermute | solution.py:392
  25.7 0.1 select_n.20
  25.8 0.6 collective-permute-start.2
  26.4 1.5 collective-permute-start.3
  27.9 0.5 collective-permute-start.4
  28.4 1.0 slice_reduce_fusion
  29.4 0.1 reshape_squeeze.6.rows
  29.4 0.1 reshape_squeeze.7.cols
  29.6 0.1 broadcast_compare_fusion
  29.6 0.0 copy-start.2
  29.6 2.3 %copy-done.2 = bf16[1,256,8192]{2,1,0:T(8,128)(2,1)S(1)} copy-done((bf16[1,256,8192]{2,1,0:T(8,128)(2,1)S(1)}, bf16[1,256,8192]{2,1,0:T(8,128)(2,1)}, u32[]{:S(2)}) %copy-start.2) | copy-done | bytes 4194328
  32.0 0.0 copy-start.3
  32.0 0.9 copy-done.3
  32.9 0.0 copy-start.4
  32.9 0.8 copy-done.4
  33.7 17.3 %weight_sums.1 = f32[192,128,128]{2,1,0:T(8,128)} custom-call(s32[192]{0:T(256)S(1)} %reshape_squeeze.6.rows, s32[192]{0:T(256)S(1)} %reshape_squeeze.7.cols, bf16[256,8192]{1,0:T(8,128)(2,1)S(1)} %bitcast.12, bf16[256,512]{1,0:T(8,128)(2,1)S(1)} %bitcast.14, f32[1,8192]{1,0:T(1,128)S(1)} %copy-done.4), custom_call_target="tpu_custom_call" | custom-call | flops 2147483648 | bytes 18874368 | tf_op jit(solution)/shard_map/weight_sums/pallas_call | solution.py:59
  51.0 0.0 copy-start
  51.0 5.1 %copy-done = f32[192,128,128]{2,1,0:T(8,128)S(1)} copy-done((f32[192,128,128]{2,1,0:T(8,128)S(1)}, f32[192,128,128]{2,1,0:T(8,128)}, u32[]{:S(2)}) %copy-start) | copy-done | bytes 12582936
  56.1 0.0 copy-start.6
  56.1 88.4 %owner_sums.1 = f32[12,128,128]{2,1,0:T(8,128)S(1)} custom-call(f32[16,12,128,128]{3,2,1,0:T(8,128)S(1)} %bitcast.9), custom_call_target="tpu_custom_call" | custom-call | flops 10000000 | bytes 262144000 | tf_op jit(solution)/shard_map/owner_sums/pallas_call | solution.py:349
  144.5 0.0 copy-done.6
  144.5 0.3 multiply_reduce_fusion
  144.7 0.6 pad.9.value_ref
  145.4 8.1 %share_sums.1 = f32[16,16,128]{2,1,0:T(8,128)} custom-call(f32[16,128]{1,0:T(8,128)} %pad.9.value_ref), custom_call_target="tpu_custom_call" | custom-call | bytes 10485760 | tf_op jit(solution)/shard_map/share_sums/pallas_call | solution.py:194
  153.5 0.9 broadcast_in_dim.53
  154.4 0.2 select_reduce_fusion
  154.6 1.3 dynamic-slice_divide_fusion
  155.9 0.1 select_reduce_fusion.1.slot_of
  156.0 0.0 collective-permute-done.4.gain_ref
  156.0 0.0 collective-permute-done.3.grad_ref
  156.0 0.0 collective-permute-done.2.x_ref
  156.0 0.0 all-gather.2.cloned.1.call-done.tiles_ref
  156.0 0.0 copy-start.1
  156.0 2.8 %copy-done.1 = bf16[192,128,128]{2,1,0:T(8,128)(2,1)S(1)} copy-done((bf16[192,128,128]{2,1,0:T(8,128)(2,1)S(1)}, bf16[192,128,128]{2,1,0:T(8,128)(2,1)}, u32[]{:S(2)}) %copy-start.1) | copy-done | bytes 6291480
  158.8 23.5 %input_part.1 = bf16[256,8192]{1,0:T(8,128)(2,1)} custom-call(s32[256]{0:T(256)S(1)} %select_reduce_fusion.1.slot_of, bf16[256,8192]{1,0:T(8,128)(2,1)} %collective-permute-done.2.x_ref, bf16[256,512]{1,0:T(8,128)(2,1)S(1)} %collective-permute-done.3.grad_ref, f32[1,8192]{1,0:T(1,128)S(1)} %collective-permute-done.4.gain_ref, ...), custom_call_target="tpu_custom_call" | custom-call | flops 2147483648 | bytes 10485760 | tf_op jit(solution)/shard_map/input_part/pallas_call | solution.py:134
  182.3 0.9 copy.10
  (2 shorter events, 0.0 us)
Async XLA Ops:
  7.2 148.9 %all-gather.2.cloned.1.call-start = ((), (), s32[]{:S(2)}) async-start(), calls=%async_computation | async-start | bytes 6684672 | tf_op jit(solution)/shard_map/all_gather | solution.py:404
  7.2 13.9 %collective-permute-start = (bf16[12,128,128]{2,1,0:T(8,128)(2,1)}, bf16[12,128,128]{2,1,0:T(8,128)(2,1)S(1)}, u32[]{:S(2)}, u32[]{:S(2)}) collective-permute-start(bf16[12,128,128]{2,1,0:T(8,128)(2,1)} %bitcast.17), channel_id=1, source_target_pairs={{0,16},{16,0},{1,17},{17,1},{2,18},{18,2},{3,19},{19,3},{4,20},{20... | collective-permute-start | bytes 1179656 | tf_op jit(solution)/shard_map/ppermute | solution.py:392
  21.1 0.7 copy-start.5
  21.8 3.8 %collective-permute-start.1 = (s32[16,2,12]{2,1,0:T(2,128)S(1)}, s32[16,2,12]{2,1,0:T(2,128)S(1)}, u32[]{:S(2)}, u32[]{:S(2)}) collective-permute-start(s32[16,2,12]{2,1,0:T(2,128)S(1)} %slice.23), channel_id=1, source_target_pairs={{0,16},{16,0},{1,17},{17,1},{2,18},{18,2},{3,19},{19,3},{4,20},{20... | collective-permute-start | bytes 4616 | tf_op jit(solution)/shard_map/ppermute | solution.py:392
  25.8 130.2 %collective-permute-start.2 = (bf16[256,8192]{1,0:T(8,128)(2,1)}, bf16[256,8192]{1,0:T(8,128)(2,1)}, u32[]{:S(2)}, u32[]{:S(2)}) collective-permute-start(bf16[256,8192]{1,0:T(8,128)(2,1)} %bitcast.11), channel_id=1, source_target_pairs={{0,16},{16,0},{1,17},{17,1},{2,18},{18,2},{3,19},{19,3},{4,20},{20... | collective-permute-start | bytes 12582920 | tf_op jit(solution)/shard_map/ppermute | solution.py:392
  26.4 129.6 %collective-permute-start.3 = (bf16[256,512]{1,0:T(8,128)(2,1)}, bf16[256,512]{1,0:T(8,128)(2,1)S(1)}, u32[]{:S(2)}, u32[]{:S(2)}) collective-permute-start(bf16[256,512]{1,0:T(8,128)(2,1)} %bitcast.13), channel_id=1, source_target_pairs={{0,16},{16,0},{1,17},{17,1},{2,18},{18,2},{3,19},{19,3},{4,20},{20... | collective-permute-start | bytes 786440 | tf_op jit(solution)/shard_map/ppermute | solution.py:392
  27.9 128.1 %collective-permute-start.4 = (f32[1,8192]{1,0:T(1,128)}, f32[1,8192]{1,0:T(1,128)S(1)}, u32[]{:S(2)}, u32[]{:S(2)}) collective-permute-start(f32[1,8192]{1,0:T(1,128)} %gain_ref.1), channel_id=1, source_target_pairs={{0,16},{16,0},{1,17},{17,1},{2,18},{18,2},{3,19},{19,3},{4,20},{20... | collective-permute-start | bytes 98312 | tf_op jit(solution)/shard_map/ppermute | solution.py:392
  29.6 2.3 %copy-start.2 = (bf16[1,256,8192]{2,1,0:T(8,128)(2,1)S(1)}, bf16[1,256,8192]{2,1,0:T(8,128)(2,1)}, u32[]{:S(2)}) copy-start(bf16[1,256,8192]{2,1,0:T(8,128)(2,1)} %param.6) | copy-start | bytes 12582916
  32.0 0.9 copy-start.3
  32.9 0.8 copy-start.4
  51.0 5.1 %copy-start = (f32[192,128,128]{2,1,0:T(8,128)S(1)}, f32[192,128,128]{2,1,0:T(8,128)}, u32[]{:S(2)}) copy-start(f32[192,128,128]{2,1,0:T(8,128)} %weight_sums.1) | copy-start | bytes 37748740
  56.1 88.4 %copy-start.6 = (bf16[1,12,128,128]{3,2,1,0:T(8,128)(2,1)S(1)}, bf16[1,12,128,128]{3,2,1,0:T(8,128)(2,1)}, u32[]{:S(2)}) copy-start(bf16[1,12,128,128]{3,2,1,0:T(8,128)(2,1)} %param.9) | copy-start | bytes 1179652
  156.0 2.8 %copy-start.1 = (bf16[192,128,128]{2,1,0:T(8,128)(2,1)S(1)}, bf16[192,128,128]{2,1,0:T(8,128)(2,1)}, u32[]{:S(2)}) copy-start(bf16[192,128,128]{2,1,0:T(8,128)(2,1)} %all-gather.2.cloned.1.call-done.tiles_ref) | copy-start | bytes 18874372
Sparse Core Ops, SparseCore 0:
  22.0 73.0 all-gather.1
